TPU v7x, 32 devices: a whole 2x2x4 slice. The times are simulated.
32 devices in a mesh: fsdp: 8 (over y, x, core), seq: 4 (over z).
Axes of the slice: x: 2, y: 2, z: 4, core: 2. Of those that a mesh axis runs over, the one named last changes fastest.
Arguments:
- tokens: bfloat16 [24, 1024, 768], P('fsdp', 'seq'), may hold values from -6 to 6
- lengths: int32 [24, 10], P('fsdp'), may hold values from 0 to 1024, as said below
- pictures: int32 [24, 1024], P('fsdp', 'seq'), may hold values from 0 to 8, as said below
- first_gain: bfloat16 [768], P('fsdp'), may hold values from 0.5 to 1.5
- mix_weight: bfloat16 [768, 2304], P('fsdp'), may hold values from -0.21875 to 0.21875
- query_gain: bfloat16 [768], P('fsdp'), may hold values from 0.796875 to 2
- key_gain: bfloat16 [768], P('fsdp'), may hold values from 0.796875 to 2
- out_weight: bfloat16 [768, 768], P('fsdp'), may hold values from -1.75 to 1.75
- second_gain: bfloat16 [768], P('fsdp'), may hold values from 0.5 to 1.5
- up_weight: bfloat16 [768, 3072], P('fsdp'), may hold values from -0.21875 to 0.21875
- down_weight: bfloat16 [3072, 768], P('fsdp'), may hold values from -0.109375 to 0.109375
- cotangent: bfloat16 [24, 1024, 768], P('fsdp', 'seq'), may hold values from -6 to 6
Outputs:
- output: bfloat16 [24, 1024, 768], P('fsdp', 'seq')
- input_grad: bfloat16 [24, 1024, 768], P('fsdp', 'seq')
- first_gain_grad: float32 [768], P('fsdp')
- mix_weight_grad: float32 [768, 2304], P('fsdp')
- query_gain_grad: float32 [768], P('fsdp')
- key_gain_grad: float32 [768], P('fsdp')
- out_weight_grad: float32 [768, 768], P('fsdp')
- second_gain_grad: float32 [768], P('fsdp')
- up_weight_grad: float32 [768, 3072], P('fsdp')
- down_weight_grad: float32 [3072, 768], P('fsdp')
Inputs may be any that keep to these rules, and one draw needn't show every extreme that they name: In each row the nonzero lengths come first, each 100 or more, and sum to 922 or more and 1024 or less; later entries are 0. Rows whose index is a multiple of 8 hold one picture of 1024 patches; rows whose index leaves 1 after division by 8 hold (922) // 100 pictures. Slot s of a row holds the number (from 0, in the order of lengths) of the picture whose patches cover s when the row's pictures are laid end to end by lengths; slots after the last picture hold the last picture's number. Numbers never fall along a row.
All inputs are finite; a program needn't handle non-finite values.
Results may differ from a plain program's by a relative error of at most 0.017.
Values may be sent and summed in bfloat16 or wider, within the bound.
A program may use at most 128 MiB of HBM per device.

v0:
```python
import jax
import jax.numpy as jnp
from jax import lax
from jax.sharding import PartitionSpec as P

HEADS = 12


EPSILON = 1e-06


def norm_rows(values, gain_row):
    center = values - jnp.mean(values, axis=-1, keepdims=True)
    spread = jnp.mean(center * center, axis=-1, keepdims=True)
    return center * lax.rsqrt(spread + EPSILON) * gain_row


def head_norms(query_raw, key_raw, query_scale, key_scale):
    return (norm_rows(query_raw, query_scale), norm_rows(key_raw, key_scale))


def gelu_exact(values):
    return jax.nn.gelu(values, approximate=False)


def key_mask(lower_block, upper_block, key_count):
    key_place = jnp.arange(key_count)
    return (key_place[None, :] >= lower_block[:, None]) & (
        key_place[None, :] < upper_block[:, None]
    )


def block_scores(query_block, keys_block, allowed, factor):
    scores = (
        jnp.einsum("qhc,khc->hqk", query_block, keys_block, preferred_element_type=jnp.float32)
        * factor
    )
    return jnp.where(allowed[None], scores, -jnp.inf)


def block_terms(query_block, grad_block, keys_block, values_block, allowed, log_total, factor):
    scores = block_scores(query_block, keys_block, allowed, factor)
    soft_weights = jnp.exp(scores - log_total[..., None])
    soft_grad = jnp.einsum(
        "qhc,khc->hqk", grad_block, values_block, preferred_element_type=jnp.float32
    )
    return (soft_weights, soft_grad)


def forward_row(queries, keys_row, values_row, lower_row, upper_row):
    length = keys_row.shape[0]
    heads_here = queries.shape[1]
    head_size = queries.shape[2]
    block_rows = min(512, length)
    block_count = length // block_rows
    factor = head_size ** (-0.5)

    def forward_one_block(inputs):
        query_block, lower_block, upper_block = inputs
        allowed = key_mask(lower_block, upper_block, length)
        scores = block_scores(query_block, keys_row, allowed, factor)
        running_max = jnp.max(scores, axis=-1, keepdims=True)
        log_total = (
            running_max + jnp.log(jnp.sum(jnp.exp(scores - running_max), axis=-1, keepdims=True))
        )[..., 0]
        soft_weights = jnp.exp(scores - log_total[..., None]).astype(jnp.bfloat16)
        attended = jnp.einsum(
            "hqk,khc->qhc", soft_weights, values_row, preferred_element_type=jnp.float32
        )
        return (attended.astype(jnp.bfloat16), log_total)

    attended, log_totals = lax.map(
        forward_one_block,
        (
            queries.reshape(block_count, block_rows, heads_here, head_size),
            lower_row.reshape(block_count, block_rows),
            upper_row.reshape(block_count, block_rows),
        ),
    )
    return (attended.reshape(length, heads_here, head_size), log_totals)


def backward_row(queries, keys_row, values_row, lower_row, upper_row, log_totals, grad_row):
    length = keys_row.shape[0]
    heads_here = queries.shape[1]
    head_size = queries.shape[2]
    block_rows = min(512, length)
    block_count = length // block_rows
    factor = head_size ** (-0.5)

    def backward_one_block(running, inputs):
        key_grad, value_grad = running
        query_block, lower_block, upper_block, log_total, grad_block = inputs
        allowed = key_mask(lower_block, upper_block, length)
        soft_weights, soft_grad = block_terms(
            query_block, grad_block, keys_row, values_row, allowed, log_total, factor
        )
        inner_sum = jnp.sum(soft_weights * soft_grad, axis=-1, keepdims=True)
        score_grad = (soft_weights * (soft_grad - inner_sum)).astype(jnp.bfloat16)
        query_grad = (
            jnp.einsum("hqk,khc->qhc", score_grad, keys_row, preferred_element_type=jnp.float32)
            * factor
        )
        key_grad = (
            key_grad
            + jnp.einsum(
                "hqk,qhc->khc", score_grad, query_block, preferred_element_type=jnp.float32
            )
            * factor
        )
        value_grad = value_grad + jnp.einsum(
            "hqk,qhc->khc",
            soft_weights.astype(jnp.bfloat16),
            grad_block,
            preferred_element_type=jnp.float32,
        )
        return ((key_grad, value_grad), query_grad)

    empty_grad = jnp.zeros((length, heads_here, head_size), jnp.float32)
    block_inputs = (
        queries.reshape(block_count, block_rows, heads_here, head_size),
        lower_row.reshape(block_count, block_rows),
        upper_row.reshape(block_count, block_rows),
        log_totals,
        grad_row.reshape(block_count, block_rows, heads_here, head_size),
    )
    (key_grad, value_grad), query_grad = lax.scan(
        backward_one_block, (empty_grad, empty_grad), block_inputs
    )
    return (query_grad.reshape(length, heads_here, head_size), key_grad, value_grad)


def local(
    tokens,
    lengths,
    pictures,
    first_gain,
    mix_weight,
    query_gain,
    key_gain,
    out_weight,
    second_gain,
    up_weight,
    down_weight,
    cotangent,
):
    seq_group = lax.axis_size("seq")
    row_count, seq_local, model_width = tokens.shape
    per_device = HEADS // seq_group
    attn_full = (
        lax.all_gather(first_gain, "fsdp", axis=0, tiled=True),
        lax.all_gather(mix_weight, "fsdp", axis=0, tiled=True),
        lax.all_gather(query_gain, "fsdp", axis=0, tiled=True),
        lax.all_gather(key_gain, "fsdp", axis=0, tiled=True),
        lax.all_gather(out_weight, "fsdp", axis=0, tiled=True),
    )
    mlp_full = (
        lax.all_gather(second_gain, "fsdp", axis=0, tiled=True),
        lax.all_gather(up_weight, "fsdp", axis=0, tiled=True),
        lax.all_gather(down_weight, "fsdp", axis=0, tiled=True),
    )
    gain_first, mix_matrix, gain_query, gain_key, out_matrix = attn_full
    gain_second, up_matrix, down_matrix = mlp_full
    row_ids = lax.all_gather(pictures, "seq", axis=1, tiled=True)
    length = row_ids.shape[1]
    starts = jnp.cumsum(lengths, axis=1) - lengths
    picture_slot = jnp.arange(lengths.shape[1])
    chosen = (row_ids[:, :, None] == picture_slot[None, None, :]).astype(jnp.int32)
    lower_bound = jnp.sum(chosen * starts[:, None, :], axis=2)
    upper_bound = lower_bound + jnp.sum(chosen * lengths[:, None, :], axis=2)
    position = lax.axis_index("seq") * seq_local + jnp.arange(seq_local)
    valid_slot = (position[None, :] < jnp.sum(lengths, axis=1)[:, None]).astype(jnp.float32)
    inputs = tokens.astype(jnp.float32)
    normed, first_pull = jax.vjp(norm_rows, inputs, gain_first.astype(jnp.float32))
    normed_low = normed.astype(jnp.bfloat16)
    mixed_all = jnp.einsum(
        "rsd,de->rse", normed_low, mix_matrix, preferred_element_type=jnp.float32
    )
    mixed_parts = mixed_all.reshape(row_count, seq_local, 3, HEADS, -1)
    head_size = mixed_parts.shape[-1]
    query_scale = gain_query.astype(jnp.float32).reshape(HEADS, head_size)
    key_scale = gain_key.astype(jnp.float32).reshape(HEADS, head_size)
    (query_norm, key_norm), head_pull = jax.vjp(
        head_norms, mixed_parts[:, :, 0], mixed_parts[:, :, 1], query_scale, key_scale
    )

    def to_groups(array):
        return array.astype(jnp.bfloat16).reshape(
            row_count, seq_local, seq_group, per_device * head_size
        )

    def to_heads(array):
        return array.reshape(row_count, length, per_device, head_size)

    exchanged = (
        lax.all_to_all(to_groups(query_norm), "seq", split_axis=2, concat_axis=1, tiled=True),
        lax.all_to_all(to_groups(key_norm), "seq", split_axis=2, concat_axis=1, tiled=True),
        lax.all_to_all(
            to_groups(mixed_parts[:, :, 2]), "seq", split_axis=2, concat_axis=1, tiled=True
        ),
    )
    queries = to_heads(exchanged[0])
    keys_all = to_heads(exchanged[1])
    values_all = to_heads(exchanged[2])

    def forward_one(inputs_row):
        return forward_row(
            inputs_row[0], inputs_row[1], inputs_row[2], inputs_row[3], inputs_row[4]
        )

    attended_heads, log_totals = lax.map(
        forward_one, (queries, keys_all, values_all, lower_bound, upper_bound)
    )
    returned = lax.all_to_all(
        attended_heads.reshape(row_count, length, 1, per_device * head_size),
        "seq",
        split_axis=1,
        concat_axis=2,
        tiled=True,
    )
    attended = returned.reshape(row_count, seq_local, model_width)
    middle = inputs + jnp.einsum(
        "rsd,de->rse", attended, out_matrix, preferred_element_type=jnp.float32
    )
    second, second_pull = jax.vjp(norm_rows, middle, gain_second.astype(jnp.float32))
    second_low = second.astype(jnp.bfloat16)
    hidden_pre = jnp.einsum(
        "rsd,df->rsf", second_low, up_matrix, preferred_element_type=jnp.float32
    )
    hidden, gelu_pull = jax.vjp(gelu_exact, hidden_pre)
    hidden_low = hidden.astype(jnp.bfloat16)
    result = middle + jnp.einsum(
        "rsf,fd->rsd", hidden_low, down_matrix, preferred_element_type=jnp.float32
    )
    output = result.astype(jnp.bfloat16)
    grad_out = cotangent.astype(jnp.float32) * valid_slot[..., None]
    grad_low = grad_out.astype(jnp.bfloat16)
    down_grad = jnp.einsum("rsf,rsd->fd", hidden_low, grad_low, preferred_element_type=jnp.float32)
    hidden_grad = jnp.einsum(
        "rsd,fd->rsf", grad_low, down_matrix, preferred_element_type=jnp.float32
    )
    (pre_grad,) = gelu_pull(hidden_grad)
    pre_low = pre_grad.astype(jnp.bfloat16)
    up_grad = jnp.einsum("rsd,rsf->df", second_low, pre_low, preferred_element_type=jnp.float32)
    second_grad = jnp.einsum("rsf,df->rsd", pre_low, up_matrix, preferred_element_type=jnp.float32)
    middle_part, gain_second_grad = second_pull(second_grad)
    middle_grad = grad_out + middle_part
    mlp_sums = (
        lax.psum_scatter(gain_second_grad, "fsdp", scatter_dimension=0, tiled=True),
        lax.psum_scatter(up_grad, "fsdp", scatter_dimension=0, tiled=True),
        lax.psum_scatter(down_grad, "fsdp", scatter_dimension=0, tiled=True),
    )
    branch_low = middle_grad.astype(jnp.bfloat16)
    out_grad = jnp.einsum("rsd,rse->de", attended, branch_low, preferred_element_type=jnp.float32)
    attended_grad = jnp.einsum(
        "rse,de->rsd", branch_low, out_matrix, preferred_element_type=jnp.float32
    ).astype(jnp.bfloat16)
    grad_heads = lax.all_to_all(
        attended_grad.reshape(row_count, seq_local, seq_group, per_device * head_size),
        "seq",
        split_axis=2,
        concat_axis=1,
        tiled=True,
    )
    grad_heads = to_heads(grad_heads)

    def backward_one(inputs_row):
        return backward_row(
            inputs_row[0],
            inputs_row[1],
            inputs_row[2],
            inputs_row[3],
            inputs_row[4],
            inputs_row[5],
            inputs_row[6],
        )

    query_grad, key_grad, value_grad = lax.map(
        backward_one,
        (queries, keys_all, values_all, lower_bound, upper_bound, log_totals, grad_heads),
    )

    def to_rows(array):
        return array.astype(jnp.bfloat16).reshape(row_count, length, 1, per_device * head_size)

    sent_back = (
        lax.all_to_all(to_rows(query_grad), "seq", split_axis=1, concat_axis=2, tiled=True),
        lax.all_to_all(to_rows(key_grad), "seq", split_axis=1, concat_axis=2, tiled=True),
        lax.all_to_all(to_rows(value_grad), "seq", split_axis=1, concat_axis=2, tiled=True),
    )

    def to_tokens(array):
        return array.astype(jnp.float32).reshape(row_count, seq_local, HEADS, head_size)

    query_back = to_tokens(sent_back[0])
    key_back = to_tokens(sent_back[1])
    value_back = to_tokens(sent_back[2])
    query_raw_grad, key_raw_grad, query_scale_grad, key_scale_grad = head_pull(
        (query_back, key_back)
    )
    mixed_grad = (
        jnp.stack([query_raw_grad, key_raw_grad, value_back], axis=2)
        .reshape(row_count, seq_local, 3 * model_width)
        .astype(jnp.bfloat16)
    )
    mix_grad = jnp.einsum("rsd,rse->de", normed_low, mixed_grad, preferred_element_type=jnp.float32)
    normed_grad = jnp.einsum(
        "rse,de->rsd", mixed_grad, mix_matrix, preferred_element_type=jnp.float32
    )
    input_part, gain_first_grad = first_pull(normed_grad)
    input_grad = (middle_grad + input_part).astype(jnp.bfloat16)
    attn_sums = (
        lax.psum_scatter(gain_first_grad, "fsdp", scatter_dimension=0, tiled=True),
        lax.psum_scatter(mix_grad, "fsdp", scatter_dimension=0, tiled=True),
        lax.psum_scatter(
            query_scale_grad.reshape(model_width), "fsdp", scatter_dimension=0, tiled=True
        ),
        lax.psum_scatter(
            key_scale_grad.reshape(model_width), "fsdp", scatter_dimension=0, tiled=True
        ),
        lax.psum_scatter(out_grad, "fsdp", scatter_dimension=0, tiled=True),
    )
    totals = (
        lax.psum(attn_sums[0].astype(jnp.bfloat16), "seq").astype(jnp.float32),
        lax.psum(attn_sums[1].astype(jnp.bfloat16), "seq").astype(jnp.float32),
        lax.psum(attn_sums[2].astype(jnp.bfloat16), "seq").astype(jnp.float32),
        lax.psum(attn_sums[3].astype(jnp.bfloat16), "seq").astype(jnp.float32),
        lax.psum(attn_sums[4].astype(jnp.bfloat16), "seq").astype(jnp.float32),
        lax.psum(mlp_sums[0].astype(jnp.bfloat16), "seq").astype(jnp.float32),
        lax.psum(mlp_sums[1].astype(jnp.bfloat16), "seq").astype(jnp.float32),
        lax.psum(mlp_sums[2].astype(jnp.bfloat16), "seq").astype(jnp.float32),
    )
    gains_first_out = totals[0]
    mix_out = totals[1]
    query_out = totals[2]
    key_out = totals[3]
    outw_out = totals[4]
    gains_second_out = totals[5]
    up_out = totals[6]
    down_out = totals[7]
    return (
        output,
        input_grad,
        gains_first_out,
        mix_out,
        query_out,
        key_out,
        outw_out,
        gains_second_out,
        up_out,
        down_out,
    )


def solution(mesh):
    return jax.shard_map(
        local,
        mesh=mesh,
        in_specs=(
            P("fsdp", "seq", None),
            P("fsdp", None),
            P("fsdp", "seq"),
            P("fsdp"),
            P("fsdp", None),
            P("fsdp"),
            P("fsdp"),
            P("fsdp", None),
            P("fsdp"),
            P("fsdp", None),
            P("fsdp", None),
            P("fsdp", "seq", None),
        ),
        out_specs=(
            P("fsdp", "seq", None),
            P("fsdp", "seq", None),
            P("fsdp"),
            P("fsdp", None),
            P("fsdp"),
            P("fsdp"),
            P("fsdp", None),
            P("fsdp"),
            P("fsdp", None),
            P("fsdp", None),
        ),
        check_vma=False,
    )
```

profile of v0, /device:TPU:0, one launch (start us, length us, event | category | flops | bytes accessed | tf_op | source)
XLA Modules:
  0.0 1014.5 jit_solution(9955325463360631227)
XLA Ops:
  13.3 16.2 %all-reduce.9 = (bf16[768]{0:T(1024)(128)(2,1)S(1)}, bf16[768]{0:T(1024)(128)(2,1)S(1)}, bf16[768]{0:T(1024)(128)(2,1)S(1)}, bf16[768]{0:T(1024)(128)(2,1)}) all-reduce(bf16[768]{0:T(1024)(128)(2,1)S(1)} %dynamic-update-slice, bf16[768]{0:T(1024)(128)(2,1)S(1)} %dynamic-update-slice.1, ...), channel_id=1, replica_groups=mesh['fsdp'=8,'seq'=4] {'fsdp'}, use_global_device_ids=true, to_apply=%add | all-reduce | flops 3072 | bytes 12288
  32.6 14.2 %all-gather.5.cloned.1.call-done = bf16[768,2304]{1,0:T(8,128)(2,1)} async-done(((bf16[96,2304]{1,0:T(8,128)(2,1)}), bf16[768,2304]{1,0:T(8,128)(2,1)}) %all-gather.5.cloned.1.call-update) | async-done | bytes 3538960 | tf_op jit(solution)/shard_map/all_gather | solution.py:152
  65.2 25.8 %all-to-all-done.1 = bf16[3,256,4,192]{1,3,0,2:T(8,128)(2,1)S(1)} async-done(((bf16[3,256,4,192]{1,3,0,2:T(8,128)(2,1)}), bf16[3,256,4,192]{1,3,0,2:T(8,128)(2,1)S(1)}, u32[]{:S(2)}, u32[]{:S(2)}) %all-to-all-start.1) | async-done | bytes 1179680 | tf_op jit(solution)/shard_map/all_to_all | solution.py:197
  98.2 24.4 %all-to-all-done = bf16[3,256,4,192]{1,3,0,2:T(8,128)(2,1)S(1)} async-done(((bf16[3,256,4,192]{1,3,0,2:T(8,128)(2,1)}), bf16[3,256,4,192]{1,3,0,2:T(8,128)(2,1)S(1)}, u32[]{:S(2)}, u32[]{:S(2)}) %all-to-all-start) | async-done | bytes 1179680 | tf_op jit(solution)/shard_map/all_to_all | solution.py:196
  128.6 31.6 %all_gather.30 = s32[3,1024]{1,0:T(4,128)S(1)} all-gather(s32[3,256]{1,0:T(4,128)S(1)} %copy-done.76), channel_id=1, replica_groups=mesh['fsdp'=8,'seq'=4] {'seq'}, dimensions={1}, use_global_device_ids=true | all-gather | bytes 15360 | tf_op jit(solution)/shard_map/all_gather | solution.py:164
  174.7 52.2 %while.54 = (s32[]{:T(128)}, bf16[3,1024,3,64]{1,3,2,0:T(8,128)(2,1)}, f32[3,2,3,512]{3,2,1,0:T(4,128)}, bf16[3,1024,3,64]{1,3,2,0:T(8,128)(2,1)}, s32[3,1024]{1...) while((s32[]{:T(128)}, ...), condition=%wide.region_14.15_spmd, body=%wide.region_9.14_spmd.sunk | while | flops 421624320 | bytes 28577076 | solution.py:211
  178.0 11.5 %while.57 = (s32[]{:T(128)}, bf16[2,512,3,64]{1,3,2,0:T(8,128)(2,1)S(1)}, f32[2,3,512]{2,1,0:T(4,128)S(1)}, s32[2,512]{1,0:T(2,128)S(1)}, s32[2,512]{1,0:T(2,128...) while((s32[]{:T(128)}, ...), condition=%wide.region_13.13_spmd, body=%wide.region_10.12_spmd.sunk | while | flops 421624320 | bytes 22222956 | solution.py:72
  236.3 44.6 %all-to-all-done.3 = bf16[3,1024,1,192]{3,0,2,1:T(4,128)(2,1)} async-done(((bf16[3,1024,1,192]{3,0,2,1:T(4,128)(2,1)}), bf16[3,1024,1,192]{3,0,2,1:T(4,128)(2,1)}, u32[]{:S(2)}, u32[]{:S(2)}) %all-to-all-start.3) | async-done | bytes 1179680 | tf_op jit(solution)/shard_map/all_to_all | solution.py:214
  305.4 22.3 %multiply_convert_fusion.1 = (bf16[3,256,3072]{2,1,0:T(8,128)(2,1)}, f32[3,256,3072]{2,1,0:T(8,128)}) fusion(f32[3,256,3072]{2,1,0:T(8,128)S(1)} %get-tuple-element.588, u8[256,3072]{1,0:T(8,128)(4,1)S(1)} %get-tuple-element.451, u8[256,3072]{1,0:T(8,128)(4,1)S(1)} %get-tuple-element.450), kind=kLoop, calls=%fused_computation.83 | loop fusion | flops 165150720 | bytes 25165824 | tf_op jit(solution)/shard_map/convert_element_type | solution.py:231
  327.7 11.5 %add_convert_fusion = bf16[3,256,3072]{2,1,0:T(8,128)(2,1)S(1)} fusion(f32[3,256,3072]{2,1,0:T(8,128)} %get-tuple-element.563, f32[3,256,3072]{2,1,0:T(8,128)} %copy-done.24, bf16[3072,768]{1,0:T(8,128)(2,1)} %all-gather.11.cloned.1.call-done, bf16[3,256,768]{2,1,0:T(8,128)(2,1)S(1)} %copy-done.29, f32[3,256]{1,0:T(4,128)S(1)} %compare_convert_fusion), kind=kOutput, calls=%fused_computation.82 | convolution fusion | flops 3658678272 | bytes 29494272 | tf_op jit(solution)/shard_map/rsd,fd->rsf/dot_general | solution.py:239
  359.9 27.9 %all-to-all-done.4 = bf16[3,256,4,192]{1,3,0,2:T(8,128)(2,1)S(1)} async-done(((bf16[3,256,4,192]{1,3,0,2:T(8,128)(2,1)}), bf16[3,256,4,192]{1,3,0,2:T(8,128)(2,1)S(1)}, u32[]{:S(2)}, u32[]{:S(2)}) %all-to-all-start.4) | async-done | bytes 1179680 | tf_op jit(solution)/shard_map/all_to_all | solution.py:258
  393.1 119.0 %while.56 = (s32[]{:T(128)}, bf16[3,1024,3,64]{1,3,2,0:T(8,128)(2,1)}, bf16[3,1024,3,64]{1,3,2,0:T(8,128)(2,1)}, bf16[3,1024,3,64]{1,3,2,0:T(8,128)(2,1)}, bf16[...) while((s32[]{:T(128)}, ...), condition=%wide.region_24.25_spmd, body=%wide.region_20.24_spmd.sunk | while | flops 1032878592 | bytes 141872592 | solution.py:278
  398.8 29.5 %while.58 = (s32[]{:T(128)}, f32[1024,3,64]{0,2,1:T(8,128)}, f32[1024,3,64]{0,2,1:T(8,128)}, bf16[2,512,3,64]{1,3,2,0:T(8,128)(2,1)}, bf16[2,512,3,64]{1,3,2,0:T...) while((s32[]{:T(128)}, f32[1024,3,64]{0,2,1:T(8,128)}, ...), condition=%wide.region_23.23_spmd.clone, body=%wide.region_21.22_spmd.clone.sunk | while | flops 1032878592 | bytes 118908936 | solution.py:127
  438.4 29.5 %while.58 = (s32[]{:T(128)}, f32[1024,3,64]{0,2,1:T(8,128)}, f32[1024,3,64]{0,2,1:T(8,128)}, bf16[2,512,3,64]{1,3,2,0:T(8,128)(2,1)}, bf16[2,512,3,64]{1,3,2,0:T...) while((s32[]{:T(128)}, f32[1024,3,64]{0,2,1:T(8,128)}, ...), condition=%wide.region_23.23_spmd.clone, body=%wide.region_21.22_spmd.clone.sunk | while | flops 1032878592 | bytes 118908936 | solution.py:127
  478.1 29.5 %while.58 = (s32[]{:T(128)}, f32[1024,3,64]{0,2,1:T(8,128)}, f32[1024,3,64]{0,2,1:T(8,128)}, bf16[2,512,3,64]{1,3,2,0:T(8,128)(2,1)}, bf16[2,512,3,64]{1,3,2,0:T...) while((s32[]{:T(128)}, f32[1024,3,64]{0,2,1:T(8,128)}, ...), condition=%wide.region_23.23_spmd.clone, body=%wide.region_21.22_spmd.clone.sunk | while | flops 1032878592 | bytes 118908936 | solution.py:127
  522.5 45.1 %all-to-all-done.5 = bf16[3,1024,1,192]{3,0,2,1:T(4,128)(2,1)S(1)} async-done(((bf16[3,1024,1,192]{3,0,2,1:T(4,128)(2,1)}), bf16[3,1024,1,192]{3,0,2,1:T(4,128)(2,1)S(1)}, u32[]{:S(2)}, u32[]{:S(2)}) %all-to-all-start.5) | async-done | bytes 1179680 | tf_op jit(solution)/shard_map/all_to_all | solution.py:287
  574.7 45.2 %all-to-all-done.6 = bf16[3,1024,1,192]{3,0,2,1:T(4,128)(2,1)} async-done(((bf16[3,1024,1,192]{3,0,2,1:T(4,128)(2,1)}), bf16[3,1024,1,192]{3,0,2,1:T(4,128)(2,1)}, u32[]{:S(2)}, u32[]{:S(2)}) %all-to-all-start.6) | async-done | bytes 1179680 | tf_op jit(solution)/shard_map/all_to_all | solution.py:288
  639.3 33.2 %all-to-all-done.7 = bf16[3,1024,1,192]{3,0,2,1:T(4,128)(2,1)} async-done(((bf16[3,1024,1,192]{3,0,2,1:T(4,128)(2,1)}), bf16[3,1024,1,192]{3,0,2,1:T(4,128)(2,1)}, u32[]{:S(2)}, u32[]{:S(2)}) %all-to-all-start.7) | async-done | bytes 1179680 | tf_op jit(solution)/shard_map/all_to_all | solution.py:289
  733.2 27.9 %reduce-scatter.5.cloned.1.call-done = f32[96,2304]{1,0:T(8,128)} async-done(((f32[768,2304]{1,0:T(8,128)}), f32[96,2304]{1,0:T(8,128)}) %reduce-scatter.5.cloned.1.call-update) | async-done | bytes 884752 | tf_op jit(solution)/shard_map/reduce_scatter | solution.py:314
  763.1 78.0 %reduce-scatter.9.cloned.1.call-done = f32[96,3072]{1,0:T(8,128)} async-done(((f32[768,3072]{1,0:T(8,128)}), f32[96,3072]{1,0:T(8,128)}) %reduce-scatter.9.cloned.1.call-update) | async-done | bytes 1179664 | tf_op jit(solution)/shard_map/reduce_scatter | solution.py:250
  843.3 77.9 %reduce-scatter.11.cloned.1.call-done = f32[384,768]{1,0:T(8,128)} async-done(((f32[3072,768]{1,0:T(8,128)}), f32[384,768]{1,0:T(8,128)}) %reduce-scatter.11.cloned.1.call-update) | async-done | bytes 1179664 | tf_op jit(solution)/shard_map/reduce_scatter | solution.py:251
  933.0 25.3 %all-reduce.8 = (bf16[768]{0:T(1024)(128)(2,1)}, bf16[768]{0:T(1024)(128)(2,1)}, bf16[768]{0:T(1024)(128)(2,1)}, bf16[768]{0:T(1024)(128)(2,1)}) all-reduce(f32[768]{0:T(1024)} %get-tuple-element.462, f32[768]{0:T(1024)} %reshape.455, f32[768]{0:T(1024)} %reshape.456, ...), channel_id=2, replica_groups=mesh['fsdp'=8,'seq'=4] {'fsdp'}, use_global_device_ids=true, to_apply=%region_32.33.clone | all-reduce | flops 3072 | bytes 18432
  963.4 12.7 %all-reduce.10 = (bf16[96]{0:T(256)(128)(2,1)}, bf16[96]{0:T(256)(128)(2,1)}, bf16[96]{0:T(256)(128)(2,1)}, bf16[96]{0:T(256)(128)(2,1)}) all-reduce(bf16[96]{0:T(256)(128)(2,1)} %dynamic-slice.19, bf16[96]{0:T(256)(128)(2,1)} %dynamic-slice.18, bf16[96]{0:T(256)(128)(2,1)} %dynamic-slice.17, ...), channel_id=1, replica_groups=mesh['fsdp'=8,'seq'=4] {'seq'}, use_global_device_ids=true, to_apply=%region_33.34 | all-reduce | flops 384 | bytes 1536 | tf_op jit(solution)/shard_map/psum | solution.py:324
  984.9 16.7 %all-reduce.14.cloned.1.call-done = (bf16[96,2304]{1,0:T(8,128)(2,1)}, bf16[96,768]{1,0:T(8,128)(2,1)}, bf16[96,3072]{1,0:T(8,128)(2,1)}, bf16[384,768]{1,0:T(8,128)(2,1)}) async-done(((bf16[96,2304]{1,0:T(8,128)(2,1)}, bf16[96,768]{1,0:T(8,128)(2,1)}, bf16[96,3072]{1,0:T(8,128)(2,1)}, bf16[384,768]{1,0:T(8,128)(2,1)}), (bf16[96,2304]{1,0:T(8,128)(2,1)}, bf16[96,768]{1,0:T(8,128)(2,1)}, ...) | async-done | bytes 1769488 | tf_op jit(solution)/shard_map/psum | solution.py:325
  (646 shorter events, 438.8 us)
Async XLA Ops:
  7.2 39.6 %all-gather.5.cloned.1.call-start = ((), (), s32[]{:S(2)}) async-start(), calls=%async_computation.12 | async-start | bytes 3981312 | tf_op jit(solution)/shard_map/all_gather | solution.py:152
  57.4 33.6 %all-to-all-start.1 = ((bf16[3,256,4,192]{1,3,0,2:T(8,128)(2,1)}), bf16[3,256,4,192]{1,3,0,2:T(8,128)(2,1)S(1)}, u32[]{:S(2)}, u32[]{:S(2)}) async-start(bf16[3,256,4,192]{1,3,0,2:T(8,128)(2,1)} %copy.229), calls=%async_computation.1 | async-start | bytes 2359296 | tf_op jit(solution)/shard_map/all_to_all | solution.py:197
  91.0 31.6 %all-to-all-start = ((bf16[3,256,4,192]{1,3,0,2:T(8,128)(2,1)}), bf16[3,256,4,192]{1,3,0,2:T(8,128)(2,1)S(1)}, u32[]{:S(2)}, u32[]{:S(2)}) async-start(bf16[3,256,4,192]{1,3,0,2:T(8,128)(2,1)} %copy.225), calls=%async_computation | async-start | bytes 2359296 | tf_op jit(solution)/shard_map/all_to_all | solution.py:196
  94.5 193.1 %all-gather.7.cloned.1.call-start = ((), (), s32[]{:S(2)}) async-start(), calls=%async_computation.13 | async-start | bytes 1327104 | tf_op jit(solution)/shard_map/all_gather | solution.py:155
  122.6 48.3 %all-to-all-start.2 = ((bf16[3,256,4,192]{1,3,0,2:T(8,128)(2,1)}), bf16[3,256,4,192]{1,3,0,2:T(8,128)(2,1)}, u32[]{:S(2)}, u32[]{:S(2)}) async-start(bf16[3,256,4,192]{1,3,0,2:T(8,128)(2,1)} %copy.231), calls=%async_computation.2 | async-start | bytes 2359296 | tf_op jit(solution)/shard_map/all_to_all | solution.py:198
  126.9 165.5 %all-gather.9.cloned.1.call-start = ((), (), s32[]{:S(2)}) async-start(), calls=%async_computation.14 | async-start | bytes 5308416 | tf_op jit(solution)/shard_map/all_gather | solution.py:159
  231.0 49.9 %all-to-all-start.3 = ((bf16[3,1024,1,192]{3,0,2,1:T(4,128)(2,1)}), bf16[3,1024,1,192]{3,0,2,1:T(4,128)(2,1)}, u32[]{:S(2)}, u32[]{:S(2)}) async-start(bf16[3,1024,1,192]{3,0,2,1:T(4,128)(2,1)} %copy.234), calls=%async_computation.3 | async-start | bytes 4194304 | tf_op jit(solution)/shard_map/all_to_all | solution.py:214
  235.6 92.1 %all-gather.11.cloned.1.call-start = ((), (), s32[]{:S(2)}) async-start(), calls=%async_computation.15 | async-start | bytes 5308416 | tf_op jit(solution)/shard_map/all_gather | solution.py:160
  236.2 112.7 %copy-start.65 = (f32[3,256]{1,0:T(4,128)}, f32[3,256]{1,0:T(4,128)S(1)}, u32[]{:S(2)}) copy-start(f32[3,256]{1,0:T(4,128)S(1)} %compare_convert_fusion) | copy-start | bytes 9220
  236.3 111.8 %copy-start.52 = (f32[768]{0:T(1024)}, f32[768]{0:T(1024)S(1)}, u32[]{:S(2)}) copy-start(f32[768]{0:T(1024)S(1)} %convert_element_type.221) | copy-start | bytes 9220
  290.5 57.6 %copy-start.48 = (f32[3,256]{1,0:T(4,128)}, f32[3,256]{1,0:T(4,128)S(1)}, u32[]{:S(2)}) copy-start(f32[3,256]{1,0:T(4,128)S(1)} %broadcast_multiply_fusion.2) | copy-start | bytes 9220
  292.4 55.7 %copy-start.54 = (f32[3,256]{1,0:T(4,128)}, f32[3,256]{1,0:T(4,128)S(1)}, u32[]{:S(2)}) copy-start(f32[3,256]{1,0:T(4,128)S(1)} %fusion.97) | copy-start | bytes 9220
  356.1 31.7 %all-to-all-start.4 = ((bf16[3,256,4,192]{1,3,0,2:T(8,128)(2,1)}), bf16[3,256,4,192]{1,3,0,2:T(8,128)(2,1)S(1)}, u32[]{:S(2)}, u32[]{:S(2)}) async-start(bf16[3,256,4,192]{1,3,0,2:T(8,128)(2,1)} %copy.239), calls=%async_computation.4 | async-start | bytes 2359296 | tf_op jit(solution)/shard_map/all_to_all | solution.py:258
  516.2 51.4 %all-to-all-start.5 = ((bf16[3,1024,1,192]{3,0,2,1:T(4,128)(2,1)}), bf16[3,1024,1,192]{3,0,2,1:T(4,128)(2,1)S(1)}, u32[]{:S(2)}, u32[]{:S(2)}) async-start(bf16[3,1024,1,192]{3,0,2,1:T(4,128)(2,1)} %copy.244), calls=%async_computation.5 | async-start | bytes 4194304 | tf_op jit(solution)/shard_map/all_to_all | solution.py:287
  567.6 52.2 %all-to-all-start.6 = ((bf16[3,1024,1,192]{3,0,2,1:T(4,128)(2,1)}), bf16[3,1024,1,192]{3,0,2,1:T(4,128)(2,1)}, u32[]{:S(2)}, u32[]{:S(2)}) async-start(bf16[3,1024,1,192]{3,0,2,1:T(4,128)(2,1)} %copy.249), calls=%async_computation.6 | async-start | bytes 4194304 | tf_op jit(solution)/shard_map/all_to_all | solution.py:288
  574.7 50.1 %copy-start.38 = (bf16[3,256,4,1,192]{1,4,2,0,3:T(8,128)(2,1)S(1)}, bf16[3,256,4,1,192]{1,4,2,0,3:T(8,128)(2,1)}, u32[]{:S(2)}) copy-start(bf16[3,256,4,1,192]{1,4,2,0,3:T(8,128)(2,1)} %copy.236) | copy-start | bytes 3538948
  619.9 52.6 %all-to-all-start.7 = ((bf16[3,1024,1,192]{3,0,2,1:T(4,128)(2,1)}), bf16[3,1024,1,192]{3,0,2,1:T(4,128)(2,1)}, u32[]{:S(2)}, u32[]{:S(2)}) async-start(bf16[3,1024,1,192]{3,0,2,1:T(4,128)(2,1)} %copy.254), calls=%async_computation.7 | async-start | bytes 4194304 | tf_op jit(solution)/shard_map/all_to_all | solution.py:289
  624.7 106.8 %reduce-scatter.7.cloned.1.call-start = ((), (), s32[]{:S(2)}) async-start(), calls=%async_computation.17 | async-start | bytes 2654208 | tf_op jit(solution)/shard_map/reduce_scatter | solution.py:321
  628.5 132.6 %reduce-scatter.5.cloned.1.call-start = ((), (), s32[]{:S(2)}) async-start(), calls=%async_computation.16 | async-start | bytes 7962624 | tf_op jit(solution)/shard_map/reduce_scatter | solution.py:314
  697.3 143.8 %reduce-scatter.9.cloned.1.call-start = ((), (), s32[]{:S(2)}) async-start(), calls=%async_computation.18 | async-start | bytes 10616832 | tf_op jit(solution)/shard_map/reduce_scatter | solution.py:250
  708.7 212.5 %reduce-scatter.11.cloned.1.call-start = ((), (), s32[]{:S(2)}) async-start(), calls=%async_computation.19 | async-start | bytes 10616832 | tf_op jit(solution)/shard_map/reduce_scatter | solution.py:251
  720.2 281.5 %all-reduce.14.cloned.1.call-start = ((), (), s32[]{:S(2)}) async-start(), calls=%async_computation.20 | async-start | bytes 3538944 | tf_op jit(solution)/shard_map/psum | solution.py:325
  763.1 160.2 %copy-start.61 = (f32[768]{0:T(1024)S(1)}, f32[768]{0:T(1024)}, u32[]{:S(2)}) copy-start(f32[768]{0:T(1024)} %copy-done.59) | copy-start | bytes 9220
  929.8 51.6 %copy-start.19 = (f32[3,256,768]{2,1,0:T(8,128)S(1)}, f32[3,256,768]{2,1,0:T(8,128)}, u32[]{:S(2)}) copy-start(f32[3,256,768]{2,1,0:T(8,128)} %copy-done.18) | copy-start | bytes 7077892
  (145 other events, 697.9 us)
Sparse Core Ops, SparseCore 0:
  9.9 36.8 all-gather.4
  97.2 24.4 all-gather.6
  129.6 39.3 all-gather.8
  238.0 39.3 all-gather.10
  628.7 42.8 reduce-scatter.6
  697.4 63.6 reduce-scatter.4
  764.6 76.4 reduce-scatter.8
  844.6 76.4 reduce-scatter.10
  924.9 76.6 all-reduce.13
where the time goes:
time: 1020 us; the launch traced here: 1010 us
  waiting for transfers between devices  463 us (45%)
  matrix products  177 us (17%)
  local copies, waits for them, and re-layouts  140 us (14%)
  other arithmetic  96.1 us (9%)
  blocking collectives  85.7 us (8%)
  starting transfers between devices  34.5 us (3%)
  between operations  16.3 us (2%)
    reduce_scatter x1, waiting for transfers between devices, local(): lax.psum_scatter(up_grad, 'fsdp', scatter_dimension=0, tiled=True)  78 us
    reduce_scatter x1, waiting for transfers between devices, local(): lax.psum_scatter(down_grad, 'fsdp', scatter_dimension=0, tiled=True)  77.9 us
    all_to_all x1, waiting for transfers between devices, local(): lax.all_to_all(to_rows(key_grad), 'seq', split_axis=1, concat_axis=2, til...  45.2 us
    all_to_all x1, waiting for transfers between devices, local(): lax.all_to_all(to_rows(query_grad), 'seq', split_axis=1, concat_axis=2, t...  45.1 us
    all_to_all x1, waiting for transfers between devices, local(): lax.all_to_all(attended_heads.reshape(row_count, length, 1, per_device *...  44.6 us
    unnamed x2, blocking collectives  41.5 us
    all_to_all x1, waiting for transfers between devices, local(): lax.all_to_all(to_rows(value_grad), 'seq', split_axis=1, concat_axis=2, t...  33.2 us
    all_gather x1, blocking collectives, local(): row_ids = lax.all_gather(pictures, 'seq', axis=1, tiled=True)  31.6 us
  transfers between devices with their start and end apart: 17, of which 12 were waited for; matrix products, arithmetic and copies ran while one was open for 22% of the time, Pallas kernels for 0%

commit v1 on v0

v1 whole, which is shorter than its diff:
```python
import functools

import jax
import jax.numpy as jnp
from jax import lax
from jax.experimental import pallas as pl
from jax.experimental.pallas import tpu as pltpu
from jax.sharding import Mesh, PartitionSpec as P

HEADS = 12
HEAD = 64
EPSILON = 1e-06
BLOCK = 256
MARK = 32.0
EXP2_FACTOR = HEAD**-0.5 * 1.4426950408889634
F32 = jnp.float32
BF16 = jnp.bfloat16
VMEM_LIMIT = 56 * 1024 * 1024

SEQ = ("zp", "zq")
COLUMN = ("core", "zp", "zq")
KEEP = [
    (core * 4 + z, (z // 2) * 4 + 2 * core + z % 2) for core in range(2) for z in range(4)
]
CROSS = [
    (core * 4 + z, (z // 2) * 4 + 2 * core + 1 - z % 2) for core in range(2) for z in range(4)
]


def inverse(pairs):
    return [(target, source) for source, target in pairs]


def swap(array, name, bit=1):
    count = lax.axis_size(name)
    return lax.ppermute(array, name, [(i, i ^ bit) for i in range(count)])


def pick(array, index, axis=0):
    return lax.dynamic_index_in_dim(array, index, axis, keepdims=False)


def ordered(mine, other, place, axis):
    first = jnp.where(place == 0, mine, other)
    second = jnp.where(place == 0, other, mine)
    return jnp.concatenate([first, second], axis=axis)


def chip_bits():
    count = lax.axis_size("chip")
    bits = count.bit_length() - 1
    return bits, [(lax.axis_index("chip") >> b) & 1 for b in range(bits)]


def gather_one(block, order):
    bits, mine = chip_bits()
    done = []
    for b in order:
        other = swap(block, "chip", 1 << b)
        axis = sum(1 for d in done if d > b)
        low = jnp.where(mine[b] == 0, block, other)
        high = jnp.where(mine[b] == 0, other, block)
        block = jnp.stack([low, high], axis=axis)
        done.append(b)
    return block.reshape((1 << bits,) + block.shape[bits:])


def gather_chips(block):
    bits, _ = chip_bits()
    half = block.shape[-1] // 2 // 128 * 128
    order = list(range(bits))
    turned = order[1:] + order[:1]
    return jnp.concatenate(
        [gather_one(block[..., :half], order), gather_one(block[..., half:], turned)], axis=-1
    )


def reduce_one(parts, order):
    bits, mine = chip_bits()
    parts = parts.reshape((2,) * bits + parts.shape[1:])
    left = list(range(bits))
    for b in order:
        axis = sum(1 for d in left if d > b)
        keep = pick(parts, mine[b], axis)
        sent = pick(parts, 1 - mine[b], axis)
        parts = (keep.astype(F32) + swap(sent, "chip", 1 << b).astype(F32)).astype(BF16)
        left.remove(b)
    return parts


def reduce_chips(parts):
    bits, _ = chip_bits()
    half = parts.shape[-1] // 2 // 128 * 128
    order = list(range(bits))
    turned = order[1:] + order[:1]
    return jnp.concatenate(
        [reduce_one(parts[..., :half], order), reduce_one(parts[..., half:], turned)], axis=-1
    )


def sum_seq(array):
    rows = array.shape[0] // 4
    z = lax.axis_index(SEQ)
    parts = array.reshape(4, rows, array.shape[1])
    total = pick(parts, z).astype(F32)
    for hop in (1, 2, 3):
        total = total + swap(pick(parts, z ^ hop), SEQ, hop).astype(F32)
    total = total.astype(BF16)
    around = [total] + [swap(total, SEQ, hop) for hop in (1, 2, 3)]
    square = jnp.stack(around).reshape(2, 2, rows, array.shape[1])
    square = jnp.where(lax.axis_index("zq") == 1, square[:, ::-1], square)
    square = jnp.where(lax.axis_index("zp") == 1, square[::-1], square)
    return square.reshape(array.shape)


def group_ones(scale):
    row = lax.broadcasted_iota(jnp.int32, (128, 128), 0) // HEAD
    column = lax.broadcasted_iota(jnp.int32, (128, 128), 1) // HEAD
    return jnp.where(row == column, scale, 0.0).astype(BF16)


def group_sum(values, ones):
    high = values.astype(BF16)
    low = (values - high.astype(F32)).astype(BF16)
    return jnp.dot(high, ones, preferred_element_type=F32) + jnp.dot(
        low, ones, preferred_element_type=F32
    )


def project_kernel(x_ref, gain_ref, weight_ref, qg_ref, kg_ref, normed_ref, q_ref, k_ref, v_ref, raw_ref):
    width = q_ref.shape[1]
    x = x_ref[...].astype(F32)
    center = x - jnp.mean(x, axis=-1, keepdims=True)
    spread = jnp.mean(center * center, axis=-1, keepdims=True)
    normed = (center * lax.rsqrt(spread + EPSILON) * gain_ref[...]).astype(BF16)
    normed_ref[...] = normed
    mixed = jnp.dot(normed, weight_ref[...], preferred_element_type=F32)
    raw_ref[...] = mixed[:, : 2 * width]
    ones = group_ones(1.0 / HEAD)
    for part, (out_ref, g_ref) in enumerate(((q_ref, qg_ref), (k_ref, kg_ref))):
        for at in range(0, width, 128):
            raw = mixed[:, part * width + at : part * width + at + 128]
            c = raw - group_sum(raw, ones)
            n = c * lax.rsqrt(group_sum(c * c, ones) + EPSILON)
            out_ref[:, at : at + 128] = (n * g_ref[:, at : at + 128]).astype(BF16)
    v_ref[...] = mixed[:, 2 * width :].astype(BF16)


def project(x, gain, weight, query_gain, key_gain):
    tokens, model = x.shape
    width = weight.shape[1] // 3
    whole = lambda shape: pl.BlockSpec(shape, lambda i: (0, 0))
    rows = lambda columns: pl.BlockSpec((BLOCK, columns), lambda i: (i, 0))
    return pl.pallas_call(
        project_kernel,
        grid=(tokens // BLOCK,),
        in_specs=[
            rows(model),
            whole((1, model)),
            whole(weight.shape),
            whole((1, width)),
            whole((1, width)),
        ],
        out_specs=[rows(model), rows(width), rows(width), rows(width), rows(2 * width)],
        out_shape=[
            jax.ShapeDtypeStruct((tokens, model), BF16),
            jax.ShapeDtypeStruct((tokens, width), BF16),
            jax.ShapeDtypeStruct((tokens, width), BF16),
            jax.ShapeDtypeStruct((tokens, width), BF16),
            jax.ShapeDtypeStruct((tokens, 2 * width), F32),
        ],
        compiler_params=pltpu.CompilerParams(vmem_limit_bytes=VMEM_LIMIT),
        cost_estimate=pl.CostEstimate(
            flops=2 * tokens * model * 3 * width, bytes_accessed=tokens * model * 12, transcendentals=0
        ),
        name="project",
    )(x, gain, weight, query_gain, key_gain)


def marks(bounds_ref, length, pics, end_row):
    place = lax.broadcasted_iota(jnp.int32, (length, 128), 0)
    inside = (place >= bounds_ref[0:1, :]) & (place < bounds_ref[end_row : end_row + 1, :])
    return jnp.where(inside, MARK, 0.0)


def nt(a, b):
    return lax.dot_general(a, b, (((1,), (1,)), ((), ())), preferred_element_type=F32)


def tn(a, b):
    return lax.dot_general(a, b, (((0,), (0,)), ((), ())), preferred_element_type=F32)


def attend_kernel(pics, info_ref, q_ref, k_ref, v_ref, bounds_ref, out_ref, aug_ref, kaug, vaug):
    length = q_ref.shape[0]
    blocks = length // BLOCK
    pair = pl.program_id(0)
    lane = lax.broadcasted_iota(jnp.int32, (1, 128), 1)
    place = lane % HEAD
    key_marks = marks(bounds_ref, length, pics, 1)
    key_marks = jnp.where(place == pics, -MARK, key_marks)
    key_marks = jnp.where((place > pics) & (place < pics + 4), 1.0, key_marks).astype(BF16)
    query_marks = marks(bounds_ref, length, pics, 2)
    query_marks = jnp.where(place == pics, MARK, query_marks).astype(BF16)
    out_ref[...] = jnp.zeros_like(out_ref)
    for h in range(2):
        inside = (lane < HEAD) if h == 0 else (lane >= HEAD)
        active = info_ref[pair * 2 + h] == 1

        @pl.when(active)
        def _():
            kaug[...] = jnp.where(inside, k_ref[...], key_marks)
            vaug[...] = jnp.where(inside, v_ref[...], jnp.ones_like(v_ref))
            for b in range(blocks):
                rows = pl.ds(b * BLOCK, BLOCK)
                query = jnp.where(inside, q_ref[rows, :], query_marks[b * BLOCK : (b + 1) * BLOCK])

                def step(j, total):
                    keys = pl.ds(pl.multiple_of(j * BLOCK, BLOCK), BLOCK)
                    scores = nt(query, kaug[keys, :])
                    weights = jnp.exp2(scores * EXP2_FACTOR).astype(BF16)
                    return total + jnp.dot(weights, vaug[keys, :], preferred_element_type=F32)

                base = 6 + 2 * b
                total = lax.fori_loop(
                    info_ref[base], info_ref[base + 1], step, jnp.zeros((BLOCK, 128), F32)
                )
                result = total / pltpu.roll(total, HEAD, 1)
                old = out_ref[rows, :]
                out_ref[rows, :] = jnp.where(inside, result.astype(BF16), old)
                log_total = jnp.log(jnp.where(inside, 1.0, total)) * -(HEAD**0.5)
                first = log_total.astype(BF16)
                rest = log_total - first.astype(F32)
                middle = rest.astype(BF16)
                last = (rest - middle.astype(F32)).astype(BF16)
                other = jnp.logical_not(inside)
                query = jnp.where(other & (place == pics + 1), first, query)
                query = jnp.where(other & (place == pics + 2), middle, query)
                query = jnp.where(other & (place == pics + 3), last, query)
                aug_ref[h, rows, :] = query

        @pl.when(jnp.logical_not(active))
        def _():
            aug_ref[h] = jnp.zeros(aug_ref.shape[1:], BF16)


def attend(info, q, k, v, bounds, pics):
    length, width = q.shape
    pairs = width // 128
    column = pl.BlockSpec((length, 128), lambda p, info: (0, p))
    return pl.pallas_call(
        functools.partial(attend_kernel, pics),
        grid_spec=pltpu.PrefetchScalarGridSpec(
            num_scalar_prefetch=1,
            grid=(pairs,),
            in_specs=[column, column, column, pl.BlockSpec((8, 128), lambda p, info: (0, 0))],
            out_specs=[column, pl.BlockSpec((2, length, 128), lambda p, info: (p, 0, 0))],
            scratch_shapes=[pltpu.VMEM((length, 128), BF16), pltpu.VMEM((length, 128), BF16)],
        ),
        out_shape=[
            jax.ShapeDtypeStruct((length, width), BF16),
            jax.ShapeDtypeStruct((2 * pairs, length, 128), BF16),
        ],
        compiler_params=pltpu.CompilerParams(vmem_limit_bytes=VMEM_LIMIT),
        cost_estimate=pl.CostEstimate(
            flops=8 * length * length * width, bytes_accessed=length * width * 12, transcendentals=0
        ),
        name="attend",
    )(info, q, k, v, bounds)


def attend_back_kernel(
    pics, info_ref, aug_ref, k_ref, v_ref, out_ref, do_ref, rawq_ref, rawk_ref, qg_ref, kg_ref, bounds_ref,
    dq_ref, dk_ref, dv_ref, qgg_ref, kgg_ref, kaug, vaug, doaug, qsum, ksum, vsum,
):
    length = k_ref.shape[0]
    blocks = length // BLOCK
    pair = pl.program_id(0)
    lane = lax.broadcasted_iota(jnp.int32, (1, 128), 1)
    place = lane % HEAD
    key_marks = marks(bounds_ref, length, pics, 1)
    key_marks = jnp.where(place == pics, -MARK, key_marks)
    key_marks = jnp.where((place > pics) & (place < pics + 4), 1.0, key_marks).astype(BF16)
    value_marks = jnp.where((place == 0) | (place == 1), 1.0, 0.0).astype(BF16)
    ones = group_ones(1.0)
    inner = group_sum(do_ref[...].astype(F32) * out_ref[...].astype(F32), ones)
    inner = -pltpu.roll(inner, HEAD, 1)
    inner_high = inner.astype(BF16)
    inner_low = (inner - inner_high.astype(F32)).astype(BF16)
    zero = jnp.zeros((), BF16)
    grad_marks = jnp.where(place == 0, inner_high, jnp.where(place == 1, inner_low, zero))
    for h in range(2):
        inside = (lane < HEAD) if h == 0 else (lane >= HEAD)
        active = info_ref[pair * 2 + h] == 1
        qsum[h] = jnp.zeros((length, 128), F32)

        @pl.when(active)
        def _():
            kaug[...] = jnp.where(inside, k_ref[...], key_marks)
            vaug[...] = jnp.where(inside, v_ref[...], value_marks)
            doaug[...] = jnp.where(inside, do_ref[...], grad_marks)
            for b in range(blocks):
                keys = pl.ds(b * BLOCK, BLOCK)
                key_block = kaug[keys, :]
                value_block = vaug[keys, :]

                def step(j, sums):
                    dk, dv = sums
                    rows = pl.ds(pl.multiple_of(j * BLOCK, BLOCK), BLOCK)
                    query = aug_ref[h, rows, :]
                    grad = doaug[rows, :]
                    weights = jnp.exp2(nt(key_block, query) * EXP2_FACTOR)
                    score_grad = (weights * nt(value_block, grad)).astype(BF16)
                    dv = dv + jnp.dot(weights.astype(BF16), grad, preferred_element_type=F32)
                    dk = dk + jnp.dot(score_grad, query, preferred_element_type=F32)
                    qsum[h, rows, :] += tn(score_grad, key_block)
                    return dk, dv

                empty = jnp.zeros((BLOCK, 128), F32)
                base = 6 + 2 * blocks + 2 * b
                dk, dv = lax.fori_loop(info_ref[base], info_ref[base + 1], step, (empty, empty))
                ksum[h, keys, :] = dk
                vsum[h, keys, :] = dv

        @pl.when(jnp.logical_not(active))
        def _():
            ksum[h] = jnp.zeros((length, 128), F32)
            vsum[h] = jnp.zeros((length, 128), F32)

    left = lane < HEAD
    means = group_ones(1.0 / HEAD)
    for sums, raw_ref, g_ref, grad_ref, gain_ref in (
        (qsum, rawq_ref, qg_ref, dq_ref, qgg_ref),
        (ksum, rawk_ref, kg_ref, dk_ref, kgg_ref),
    ):
        gain_sum = jnp.zeros((1, 128), F32)
        for b in range(blocks):
            rows = pl.ds(b * BLOCK, BLOCK)
            e = jnp.where(left, sums[0, rows, :], sums[1, rows, :]) * HEAD**-0.5
            e = e.astype(BF16).astype(F32)
            raw = raw_ref[rows, :]
            c = raw - group_sum(raw, means)
            r = lax.rsqrt(group_sum(c * c, means) + EPSILON)
            n = c * r
            gain_sum = gain_sum + jnp.sum(e * n, axis=0, keepdims=True)
            t = e * g_ref[...]
            grad = r * (t - group_sum(t, means) - n * group_sum(t * n, means))
            grad_ref[rows, :] = grad.astype(BF16)
        gain_ref[...] = gain_sum
    dv_ref[...] = jnp.where(left, vsum[0], vsum[1]).astype(BF16)


def attend_back(info, aug, k, v, out, do, raw, query_gain, key_gain, bounds, pics):
    length, width = k.shape
    pairs = width // 128
    column = pl.BlockSpec((length, 128), lambda p, info: (0, p))
    gain = pl.BlockSpec((1, 128), lambda p, info: (0, p))
    return pl.pallas_call(
        functools.partial(attend_back_kernel, pics),
        grid_spec=pltpu.PrefetchScalarGridSpec(
            num_scalar_prefetch=1,
            grid=(pairs,),
            in_specs=[
                pl.BlockSpec((2, length, 128), lambda p, info: (p, 0, 0)),
                column,
                column,
                column,
                column,
                column,
                pl.BlockSpec((length, 128), lambda p, info: (0, pairs + p)),
                gain,
                gain,
                pl.BlockSpec((8, 128), lambda p, info: (0, 0)),
            ],
            out_specs=[column, column, column, gain, gain],
            scratch_shapes=[
                pltpu.VMEM((length, 128), BF16),
                pltpu.VMEM((length, 128), BF16),
                pltpu.VMEM((length, 128), BF16),
                pltpu.VMEM((2, length, 128), F32),
                pltpu.VMEM((2, length, 128), F32),
                pltpu.VMEM((2, length, 128), F32),
            ],
        ),
        out_shape=[
            jax.ShapeDtypeStruct((length, width), BF16),
            jax.ShapeDtypeStruct((length, width), BF16),
            jax.ShapeDtypeStruct((length, width), BF16),
            jax.ShapeDtypeStruct((1, width), F32),
            jax.ShapeDtypeStruct((1, width), F32),
        ],
        compiler_params=pltpu.CompilerParams(vmem_limit_bytes=VMEM_LIMIT),
        cost_estimate=pl.CostEstimate(
            flops=20 * length * length * width, bytes_accessed=length * width * 20, transcendentals=0
        ),
        name="attend_back",
    )(info, aug, k, v, out, do, raw, raw, query_gain, key_gain, bounds)


def gelu_pair(h):
    size = jnp.abs(h)
    bell = jnp.exp2(h * h * -0.7213475204444817)
    t = 1.0 / (1.0 + 0.23164189 * size)
    series = t * (0.127414796 + t * (-0.142248368 + t * (0.7107068705 + t * (-0.7265760135 + t * 0.5307027145))))
    tail = series * bell
    below = jnp.where(h < 0.0, tail, 1.0 - tail)
    return h * below, below + h * (bell * 0.3989422804014327)


def mlp_kernel(second_ref, grad_ref, up_ref, down_ref, out_ref, back_ref, upg_ref, downg_ref):
    first = pl.program_id(0) == 0

    @pl.when(first)
    def _():
        out_ref[...] = jnp.zeros_like(out_ref)
        back_ref[...] = jnp.zeros_like(back_ref)

    second = second_ref[...]
    grad = grad_ref[...]
    up = up_ref[...]
    down = down_ref[...]
    pre = jnp.dot(second, up, preferred_element_type=F32)
    hidden, slope = gelu_pair(pre)
    hidden = hidden.astype(BF16)
    out_ref[...] += jnp.dot(hidden, down, preferred_element_type=F32)
    pre_grad = (nt(grad, down) * slope).astype(BF16)
    downg_ref[...] = tn(hidden, grad).astype(BF16)
    upg_ref[...] = tn(second, pre_grad).astype(BF16)
    back_ref[...] += nt(pre_grad, up)


def mlp(second, grad, up, down):
    tokens, model = second.shape
    hidden = up.shape[1]
    tile = 512
    whole = pl.BlockSpec((tokens, model), lambda i: (0, 0))
    wide = pl.BlockSpec((model, tile), lambda i: (0, i))
    tall = pl.BlockSpec((tile, model), lambda i: (i, 0))
    return pl.pallas_call(
        mlp_kernel,
        grid=(hidden // tile,),
        in_specs=[whole, whole, wide, tall],
        out_specs=[whole, whole, wide, tall],
        out_shape=[
            jax.ShapeDtypeStruct((tokens, model), F32),
            jax.ShapeDtypeStruct((tokens, model), F32),
            jax.ShapeDtypeStruct((model, hidden), BF16),
            jax.ShapeDtypeStruct((hidden, model), BF16),
        ],
        compiler_params=pltpu.CompilerParams(vmem_limit_bytes=VMEM_LIMIT),
        cost_estimate=pl.CostEstimate(
            flops=12 * tokens * model * hidden, bytes_accessed=8 * model * hidden, transcendentals=0
        ),
        name="mlp",
    )(second, grad, up, down)


def norm_parts(values):
    center = values - jnp.mean(values, axis=-1, keepdims=True)
    spread = lax.rsqrt(jnp.mean(center * center, axis=-1, keepdims=True) + EPSILON)
    return center * spread, spread


def norm_back(upstream, n, r, gain):
    t = upstream * gain
    return (
        r * (t - jnp.mean(t, axis=-1, keepdims=True) - n * jnp.mean(t * n, axis=-1, keepdims=True)),
        jnp.sum(upstream * n, axis=0),
    )


def row_layout(lengths_row, length):
    pics = lengths_row.shape[0]
    blocks = length // BLOCK
    ends = jnp.cumsum(lengths_row)
    starts = ends - lengths_row
    live = lengths_row > 0
    last = jnp.arange(pics) == jnp.sum(live) - 1
    query_ends = jnp.where(last, length, ends)
    fill = jnp.full((HEAD - pics,), 2 * length, jnp.int32)
    lanes = lambda values: jnp.tile(jnp.concatenate([values.astype(jnp.int32), fill]), 2)
    bounds = jnp.stack([lanes(starts), lanes(ends), lanes(query_ends)] + [lanes(ends)] * 5)
    edge = jnp.arange(blocks) * BLOCK
    holds = lambda slots: (starts[None, :] <= slots[:, None]) & (slots[:, None] < query_ends[None, :])
    low = jnp.sum(jnp.where(holds(edge), starts[None, :], 0), axis=1) // BLOCK
    high = (jnp.sum(jnp.where(holds(edge + BLOCK - 1), ends[None, :], 0), axis=1) - 1) // BLOCK + 1
    at = jnp.arange(blocks)
    query_low = jnp.sum(high[None, :] <= at[:, None], axis=1)
    query_high = jnp.sum(low[None, :] <= at[:, None], axis=1)
    ranges = jnp.concatenate(
        [jnp.stack([low, high], axis=1).reshape(-1), jnp.stack([query_low, query_high], axis=1).reshape(-1)]
    )
    return bounds, ranges.astype(jnp.int32), ends[-1]


def local(
    tokens, lengths, pictures, first_gain, mix_weight, query_gain, key_gain, out_weight,
    second_gain, up_weight, down_weight, cotangent,
):
    core, zp, zq = lax.axis_index("core"), lax.axis_index("zp"), lax.axis_index("zq")
    chips = lax.axis_size("chip")
    _, part, model = tokens.shape
    length = 4 * part
    half = 2 * part
    heads_core = HEADS // 2
    width = heads_core * HEAD
    third = width // 2
    pics = lengths.shape[1]
    shard = mix_weight.shape[0]

    def spread(array):
        mine = lax.ppermute(pick(array, zq), COLUMN, KEEP)
        cross = lax.ppermute(pick(array, 1 - zq), COLUMN, CROSS)
        shared = lax.ppermute(array[2], COLUMN, KEEP)
        return ordered(mine, cross, zq, 0), shared

    def collect(array):
        first, second, shared = array[:part], array[part:half], array[half:]
        mine = lax.ppermute(jnp.where(zq == 0, first, second), COLUMN, inverse(KEEP))
        cross = lax.ppermute(jnp.where(zq == 0, second, first), COLUMN, inverse(CROSS))
        shared = lax.ppermute(shared, COLUMN, inverse(KEEP))
        return jnp.stack([jnp.where(zq == 0, mine, cross), jnp.where(zq == 0, cross, mine), shared])

    own_half, own_quarter = spread(tokens)
    row_tokens = ordered(own_half, swap(own_half, "core"), core, 0)
    shared_half = ordered(own_quarter, swap(own_quarter, "zq"), zq, 0)
    shared_tokens = ordered(shared_half, swap(shared_half, "core"), core, 0)
    grad_half, grad_quarter = spread(cotangent)

    lengths_owner = jnp.where(core == zp, lengths, swap(lengths, "core"))
    row_bounds, row_ranges, row_filled = row_layout(pick(lengths_owner, zq), length)
    shared_bounds, shared_ranges, shared_filled = row_layout(lengths_owner[2], length)
    row_info = jnp.concatenate([jnp.ones((heads_core,), jnp.int32), row_ranges])
    mine_heads = (jnp.arange(heads_core) // (heads_core // 2) == zq).astype(jnp.int32)
    shared_info = jnp.concatenate([mine_heads, shared_ranges])

    gains = jnp.concatenate([first_gain, query_gain, key_gain, second_gain])
    gains = jnp.pad(gains[None], ((0, 15), (0, 3 * width - 4 * shard)))
    mix_split = mix_weight.reshape(shard, 3, 2, width)
    mine_mix = jnp.concatenate([pick(mix_split, core, 2).reshape(shard, 3 * width), gains])
    sent_mix = jnp.concatenate([pick(mix_split, 1 - core, 2).reshape(shard, 3 * width), gains])
    other_mix = swap(sent_mix, "core")
    mix_pair = ordered(mine_mix[None], other_mix[None], core, 0).reshape(-1, 3 * width)
    mix_all = gather_chips(mix_pair).reshape(2 * chips, shard + 16, 3 * width)
    mix_half = mix_all[:, :shard].reshape(model, 3 * width)
    gains = mix_all[:, shard, : 4 * shard].reshape(2 * chips, 4, shard).astype(F32)
    gains = jnp.transpose(gains, (1, 0, 2)).reshape(4, 1, model)
    gain_first, gain_query, gain_key, gain_second = gains[0], gains[1], gains[2], gains[3]
    gain_query = pick(gain_query.reshape(2, 1, width), core)
    gain_key = pick(gain_key.reshape(2, 1, width), core)

    def gather_whole(weight):
        mine = gather_chips(weight)
        return ordered(mine[:, None], swap(mine, "core")[:, None], core, 1).reshape(-1, weight.shape[1])

    out_matrix = gather_whole(out_weight)
    up_matrix = gather_whole(up_weight)
    down_matrix = gather_whole(down_weight)

    row_normed, row_q, row_k, row_v, row_raw = project(row_tokens, gain_first, mix_half, gain_query, gain_key)
    row_out, row_aug = attend(row_info, row_q, row_k, row_v, row_bounds, pics)
    shared_normed, shared_q, shared_k, shared_v, shared_raw = project(
        shared_tokens, gain_first, mix_half, gain_query, gain_key
    )
    shared_out, shared_aug = attend(shared_info, shared_q, shared_k, shared_v, shared_bounds, pics)

    square = pick(shared_out.reshape(2, 2, part, 2, third), zq, 3)
    kept = pick(square, zq, 1)
    got = swap(pick(square, 1 - zq, 1), "zq")
    quarters = ordered(kept, got, zq, 2)
    row_halves = row_out.reshape(2, half, width)
    mine = jnp.concatenate([pick(row_halves, core), pick(quarters, core)])
    other = swap(jnp.concatenate([pick(row_halves, 1 - core), pick(quarters, 1 - core)]), "core")
    attended = ordered(mine, other, core, 1)

    inputs = jnp.concatenate([own_half, own_quarter]).astype(F32)
    middle = inputs + jnp.dot(attended, out_matrix, preferred_element_type=F32)
    n_second, r_second = norm_parts(middle)
    second = (n_second * gain_second).astype(BF16)
    row_place = core * half + jnp.arange(half)
    shared_place = (2 * core + zq) * part + jnp.arange(part)
    valid = jnp.concatenate([row_place < row_filled, shared_place < shared_filled])
    grad_low = jnp.concatenate([grad_half, grad_quarter]) * valid[:, None].astype(BF16)

    delta, second_grad, up_grad, down_grad = mlp(second, grad_low, up_matrix, down_matrix)
    output = collect((middle + delta).astype(BF16))

    middle_part, gain_second_grad = norm_back(second_grad, n_second, r_second, gain_second)
    middle_grad = grad_low.astype(F32) + middle_part
    branch = middle_grad.astype(BF16)
    attended_grad = nt(branch, out_matrix).astype(BF16)
    out_grad = tn(attended, branch).astype(BF16)

    def reduce_whole(grad):
        columns = grad.shape[1]
        split = grad.reshape(chips, 2, -1, columns)
        mine, sent = pick(split, core, 1), pick(split, 1 - core, 1)
        paired = (mine.astype(F32) + swap(sent, "core").astype(F32)).astype(BF16)
        return sum_seq(reduce_chips(paired)).astype(F32)

    up_out = reduce_whole(up_grad)
    down_out = reduce_whole(down_grad)
    outw_out = reduce_whole(out_grad)

    grad_split = attended_grad.reshape(-1, 2, width)
    mine = pick(grad_split, core, 1)
    other = swap(pick(grad_split, 1 - core, 1), "core")
    row_grad = ordered(mine[:half], other[:half], core, 0)
    quarters = ordered(mine[None, half:], other[None, half:], core, 0).reshape(2, part, 2, third)
    kept = pick(quarters, zq, 2)
    got = swap(pick(quarters, 1 - zq, 2), "zq")
    square = ordered(kept[:, None], got[:, None], zq, 1).reshape(length, 1, third)
    shared_grad = jnp.where(jnp.arange(2)[None, :, None] == zq, square, 0).reshape(length, width)

    shared_dq, shared_dk, shared_dv, shared_qgg, shared_kgg = attend_back(
        shared_info, shared_aug, shared_k, shared_v, shared_out, shared_grad, shared_raw,
        gain_query, gain_key, shared_bounds, pics,
    )
    row_dq, row_dk, row_dv, row_qgg, row_kgg = attend_back(
        row_info, row_aug, row_k, row_v, row_out, row_grad, row_raw, gain_query, gain_key, row_bounds, pics
    )
    shared_mixed = jnp.concatenate([shared_dq, shared_dk, shared_dv], axis=1)
    row_mixed = jnp.concatenate([row_dq, row_dk, row_dv], axis=1)
    square = pick(shared_mixed.reshape(2, 2, part, 3, 2, third), zq, 4)
    kept = pick(square, zq, 1)
    got = swap(pick(square, 1 - zq, 1), "zq")
    quarters = ordered(kept[:, :, :, None], got[:, :, :, None], zq, 3).reshape(half, 3 * width)

    mix_grad = tn(
        jnp.concatenate([row_normed, shared_normed]), jnp.concatenate([row_mixed, shared_mixed])
    ).astype(BF16)
    partial = nt(jnp.concatenate([row_mixed, quarters]), mix_half)
    row_partial = partial[:length].reshape(2, half, model)
    shared_partial = partial[length:].reshape(2, part, model)
    mine = jnp.concatenate([pick(row_partial, core), pick(shared_partial, core)])
    sent = jnp.concatenate([pick(row_partial, 1 - core), pick(shared_partial, 1 - core)])
    normed_grad = mine + swap(sent.astype(BF16), "core").astype(F32)
    n_first, r_first = norm_parts(inputs)
    input_part, gain_first_grad = norm_back(normed_grad, n_first, r_first, gain_first)
    input_grad = collect((middle_grad + input_part).astype(BF16))

    def place_heads(values):
        return jnp.where(jnp.arange(2)[:, None] == core, values, 0.0).reshape(model)

    gain_grads = jnp.stack(
        [gain_first_grad, place_heads(row_qgg + shared_qgg), place_heads(row_kgg + shared_kgg), gain_second_grad]
    )
    gain_grads = gain_grads.reshape(4, chips, 2 * shard).transpose(1, 0, 2).reshape(chips, 1, -1)
    gain_grads = jnp.pad(gain_grads, ((0, 0), (0, 15), (0, 3 * width - gain_grads.shape[2]))).astype(BF16)
    payload = jnp.concatenate([mix_grad.reshape(chips, 2 * shard, 3 * width), gain_grads], axis=1)
    reduced = reduce_chips(payload)
    mix_rows = reduced[: 2 * shard].reshape(2, shard, 3 * width)
    gain_rows = reduced[2 * shard :]
    other = swap(jnp.concatenate([pick(mix_rows, 1 - core), gain_rows]), "core")
    mix_columns = ordered(
        pick(mix_rows, core).reshape(shard, 3, 1, width), other[:shard].reshape(shard, 3, 1, width), core, 2
    )
    gain_rows = (gain_rows.astype(F32) + other[shard:].astype(F32)).astype(BF16)
    final = jnp.concatenate([mix_columns.reshape(2 * shard, 3 * width), gain_rows])
    spare = -final.shape[0] % 64
    final = sum_seq(jnp.pad(final, ((0, spare), (0, 0)))).astype(F32)
    mix_out = final[: 2 * shard].reshape(shard, 6 * width)
    gains_out = pick(final[2 * shard, : 8 * shard].reshape(4, 2, shard), core, 1)
    return (
        output,
        input_grad,
        gains_out[0],
        mix_out,
        gains_out[1],
        gains_out[2],
        outw_out,
        gains_out[3],
        up_out,
        down_out,
    )


def solution(mesh):
    fsdp = mesh.shape["fsdp"]
    split = Mesh(mesh.devices.reshape(fsdp // 2, 2, 2, 2), ("chip", "core", "zp", "zq"))
    rows = ("chip", "core")
    return jax.shard_map(
        local,
        mesh=split,
        in_specs=(
            P(rows, SEQ, None),
            P(rows, None),
            P(rows, SEQ),
            P(rows),
            P(rows, None),
            P(rows),
            P(rows),
            P(rows, None),
            P(rows),
            P(rows, None),
            P(rows, None),
            P(rows, SEQ, None),
        ),
        out_specs=(
            P(rows, SEQ, None),
            P(rows, SEQ, None),
            P(rows),
            P(rows, None),
            P(rows),
            P(rows),
            P(rows, None),
            P(rows),
            P(rows, None),
            P(rows, None),
        ),
        check_vma=False,
    )
```

time: 1020 us -> 690 us (0.68)
  waiting for transfers between devices: 463 us -> 93.1 us
  Pallas kernels: 0 us -> 215 us
  matrix products: 177 us -> 16.7 us
  starting transfers between devices: 34.5 us -> 171 us
  blocking collectives: 85.7 us -> 0 us
  local copies, waits for them, and re-layouts: 140 us -> 91 us
  between operations: 16.3 us -> 4.58 us
    all_to_all x8 -> x0, waiting for transfers between devices: 246 us -> none  [the longest x1 45.2 us: local(): lax.all_to_all(to_rows(key_grad), 'seq', split_axis=1, concat_axis=2, til...]
    pallas_call x0 -> x7, Pallas kernels: none -> 215 us  [the longest x2 102 us: attend_back(): pl.pallas_call(functools.partial(attend_back_kernel, pics), grid_spec=plt...]
    reduce_scatter x4 -> x0, waiting for transfers between devices: 184 us -> none  [the longest x1 78 us: local(): lax.psum_scatter(up_grad, 'fsdp', scatter_dimension=0, tiled=True)]
    ppermute x0 -> x86, starting transfers between devices: none -> 171 us  [the longest x74 153 us: swap(): return lax.ppermute(array, name, [(i, i ^ bit) for i in range(count)])]
    dot_general x54 -> x5, matrix products: 177 us -> 16.7 us  [the longest x2 8.57 us: tn(): lax.dot_general(a, b, (((0,), (0,)), ((), ())), preferred_element_type=F32)]
    ppermute x0 -> x86, waiting for transfers between devices: none -> 93.1 us  [the longest x74 86 us: swap(): return lax.ppermute(array, name, [(i, i ^ bit) for i in range(count)])]
    unnamed x2 -> x0, blocking collectives: 41.5 us -> none
    all_to_all x8 -> x0, starting transfers between devices: 33.7 us -> none  [the longest x1 4.84 us: local(): lax.all_to_all(to_rows(value_grad), 'seq', split_axis=1, concat_axis=2, t...]
  transfers between devices with their start and end apart: 17 -> 86, of which waited for: 12 -> 22; matrix products, arithmetic and copies ran while one was open for 22% -> 25% of each run, Pallas kernels for 0% -> 27%
where the time goes in v1:
time: 690 us; the launch traced here: 681 us
  Pallas kernels  215 us (31%)
  starting transfers between devices  171 us (25%)
  waiting for transfers between devices  93.1 us (13%)
  local copies, waits for them, and re-layouts  91 us (13%)
  other arithmetic  89.4 us (13%)
  matrix products  16.7 us (2%)
    ppermute x74, starting transfers between devices, swap(): return lax.ppermute(array, name, [(i, i ^ bit) for i in range(count)])  153 us
    pallas_call x2, Pallas kernels, attend_back(): pl.pallas_call(functools.partial(attend_back_kernel, pics), grid_spec=plt...  102 us
    ppermute x74, waiting for transfers between devices, swap(): return lax.ppermute(array, name, [(i, i ^ bit) for i in range(count)])  86 us
    pallas_call x2, Pallas kernels, attend(): pl.pallas_call(functools.partial(attend_kernel, pics), grid_spec=pltpu.Pr...  63.6 us
    pallas_call x1, Pallas kernels, mlp(): pl.pallas_call(mlp_kernel, grid=(hidden // tile,), in_specs=[whole, whole...  32.3 us
    squeeze x32, local copies, waits for them, and re-layouts, pick(): return lax.dynamic_index_in_dim(array, index, axis, keepdims=False)  19 us
    pallas_call x2, Pallas kernels, project(): pl.pallas_call(project_kernel, grid=(tokens // BLOCK,), in_specs=[rows(mo...  17.6 us
  transfers between devices with their start and end apart: 86, of which 22 were waited for; matrix products, arithmetic and copies ran while one was open for 25% of the time, Pallas kernels for 27%

profile of v1, /device:TPU:0, one launch (start us, length us, event | category | flops | bytes accessed | tf_op | source)
XLA Modules:
  0.0 681.3 jit_solution(7331371659453978046)
XLA Ops:
  33.3 7.7 %collective-permute-done.15 = bf16[2,96,384]{2,1,0:T(8,128)(2,1)S(1)} collective-permute-done((bf16[2,96,384]{2,1,0:T(8,128)(2,1)S(1)}, bf16[2,96,384]{2,1,0:T(8,128)(2,1)S(1)}, u32[]{:S(2)}, u32[]{:S(2)}) %collective-permute-start.15) | collective-permute-done | bytes 147488 | tf_op jit(solution)/shard_map/ppermute | solution.py:36
  61.9 13.5 %collective-permute-start.18 = (bf16[4,96,768]{2,1,0:T(8,128)(2,1)S(1)}, bf16[4,96,768]{2,1,0:T(8,128)(2,1)S(1)}, u32[]{:S(2)}, u32[]{:S(2)}) collective-permute-start(bf16[4,96,768]{2,1,0:T(8,128)(2,1)S(1)} %pad_maximum_fusion.27), channel_id=1, source_target_pairs={{0,4},{4,0},{1,5},{5,1},{2,6},{6,2},{3,7},{7,3},{8,12},{12,8},{9,1... | collective-permute-start | bytes 1769480 | tf_op jit(solution)/shard_map/ppermute | solution.py:36
  83.3 18.6 %collective-permute-start.10 = (bf16[256,768]{1,0:T(8,128)(2,1)S(1)}, bf16[256,768]{1,0:T(8,128)(2,1)S(1)}, u32[]{:S(2)}, u32[]{:S(2)}) collective-permute-start(bf16[256,768]{1,0:T(8,128)(2,1)S(1)} %collective-permute-done.2), channel_id=1, source_target_pairs={{0,1},{1,0},{2,3},{3,2},{4,5},{5,4},{6,7},{7,6},{8,9},{9,8},{10,11... | collective-permute-start | bytes 1179656 | tf_op jit(solution)/shard_map/ppermute | solution.py:36
  111.0 6.4 collective-permute-start.4
  145.2 8.9 %project.2 = (bf16[1024,768]{1,0:T(8,128)(2,1)}, bf16[1024,384]{1,0:T(8,128)(2,1)}, bf16[1024,384]{1,0:T(8,128)(2,1)}, bf16[1024,384]{1,0:T(8,128)(2,1)}, f32[1024,768]{1,0:T(8,128)}) custom-call(bf16[1024,768]{1,0:T(8,128)(2,1)} %pad_maximum_fusion.5.x_ref, f32[1,768]{1,0:T(1,128)} %squeeze.261.gain_ref, bf16[768,1152]{1,0:T(8,128)(2,1)} %bitcast.532, ...), custom_call_target="tpu_custom_call" | custom-call | flops 1811939328 | bytes 9437184 | tf_op jit(solution)/shard_map/project/pallas_call | solution.py:154
  154.1 8.7 %project.3 = (bf16[1024,768]{1,0:T(8,128)(2,1)}, bf16[1024,384]{1,0:T(8,128)(2,1)}, bf16[1024,384]{1,0:T(8,128)(2,1)}, bf16[1024,384]{1,0:T(8,128)(2,1)}, f32[1024,768]{1,0:T(8,128)}) custom-call(bf16[1024,768]{1,0:T(8,128)(2,1)} %pad_maximum_fusion.6.x_ref, f32[1,768]{1,0:T(1,128)} %squeeze.261.gain_ref, bf16[768,1152]{1,0:T(8,128)(2,1)} %bitcast.533, ...), custom_call_target="tpu_custom_call" | custom-call | flops 1811939328 | bytes 9437184 | tf_op jit(solution)/shard_map/project/pallas_call | solution.py:154
  162.8 22.6 %attend.3 = (bf16[1024,384]{1,0:T(8,128)(2,1)}, bf16[6,1024,128]{2,1,0:T(8,128)(2,1)}) custom-call(s32[22]{0:T(128)} %pad_add_fusion.5.info_ref, bf16[1024,384]{1,0:T(8,128)(2,1)} %get-tuple-element.42.q_ref, bf16[1024,384]{1,0:T(8,128)(2,1)} %get-tuple-element.43.k_ref, bf16[1024,384]{1,0:T(8,128)(2,1)} %get-tuple-element.44.v_ref, s32[8,128]{1,0:T(8,128)} %stack.292.bounds_ref), custom_call_target="tpu_custom_call" | custom-call | flops 3221225472 | bytes 4718592 | tf_op jit(solution)/shard_map/attend/pallas_call | solution.py:251
  192.9 8.5 %collective-permute-start.12 = (bf16[2,256,192]{1,2,0:T(8,128)(2,1)S(1)}, bf16[2,256,192]{1,2,0:T(8,128)(2,1)S(1)}, u32[]{:S(2)}, u32[]{:S(2)}) collective-permute-start(bf16[2,256,192]{1,2,0:T(8,128)(2,1)S(1)} %bitcast.565), channel_id=1, source_target_pairs={{0,1},{1,0},{2,3},{3,2},{4,5},{5,4},{6,7},{7,6},{8,9},{9,8},{10,11... | collective-permute-start | bytes 589832 | tf_op jit(solution)/shard_map/ppermute | solution.py:36
  201.4 41.0 %attend.2 = (bf16[1024,384]{1,0:T(8,128)(2,1)}, bf16[6,1024,128]{2,1,0:T(8,128)(2,1)}) custom-call(s32[22]{0:T(128)} %pad_add_fusion.4.info_ref, bf16[1024,384]{1,0:T(8,128)(2,1)} %get-tuple-element.38.q_ref, bf16[1024,384]{1,0:T(8,128)(2,1)} %get-tuple-element.39.k_ref, bf16[1024,384]{1,0:T(8,128)(2,1)} %get-tuple-element.40.v_ref, s32[8,128]{1,0:T(8,128)} %stack.287.bounds_ref), custom_call_target="tpu_custom_call" | custom-call | flops 3221225472 | bytes 4718592 | tf_op jit(solution)/shard_map/attend/pallas_call | solution.py:251
  271.5 32.3 %mlp.1 = (f32[768,768]{1,0:T(8,128)}, f32[768,768]{1,0:T(8,128)}, bf16[768,3072]{1,0:T(8,128)(2,1)}, bf16[3072,768]{1,0:T(8,128)(2,1)}) custom-call(bf16[768,768]{1,0:T(8,128)(2,1)} %multiply_convert_fusion.second_ref, bf16[768,768]{1,0:T(8,128)(2,1)} %maximum_multiply_fusion.grad_ref, bf16[768,3072]{1,0:T(8,128)(2,1)} %bitcast.496, bf16[3072,768]{1,0:T(8,128)(2,1)} %bitcast.495), custom_call_target="tpu_custom_call" | custom-call | flops 21743271936 | bytes 18874368 | tf_op jit(solution)/shard_map/mlp/pallas_call | solution.py:439
  330.7 6.9 %collective-permute-start.64 = (bf16[4,96,3072]{2,1,0:T(8,128)(2,1)}, bf16[4,96,3072]{2,1,0:T(8,128)(2,1)}, u32[]{:S(2)}, u32[]{:S(2)}) collective-permute-start(bf16[4,96,3072]{2,1,0:T(8,128)(2,1)} %dynamic-slice_bitcast_fusion.1), channel_id=1, source_target_pairs={{0,4},{4,0},{1,5},{5,1},{2,6},{6,2},{3,7},{7,3},{8,12},{12,8},{9,1... | collective-permute-start | bytes 7077896 | tf_op jit(solution)/shard_map/ppermute | solution.py:36
  344.0 63.5 %attend_back.2 = (bf16[1024,384]{1,0:T(8,128)(2,1)}, bf16[1024,384]{1,0:T(8,128)(2,1)}, bf16[1024,384]{1,0:T(8,128)(2,1)}, f32[1,384]{1,0:T(1,128)}, f32[1,384]{1,0:T(1,128)}) custom-call(s32[22]{0:T(128)} %pad_add_fusion.4.info_ref, bf16[6,1024,128]{2,1,0:T(8,128)(2,1)} %get-tuple-element.48.aug_ref, bf16[1024,384]{1,0:T(8,128)(2,1)} %get-tuple-element.39.k_ref, ...), custom_call_target="tpu_custom_call" | custom-call | flops 8053063680 | bytes 7864320 | tf_op jit(solution)/shard_map/attend_back/pallas_call | solution.py:358
  419.0 38.4 %attend_back.3 = (bf16[1024,384]{1,0:T(8,128)(2,1)}, bf16[1024,384]{1,0:T(8,128)(2,1)}, bf16[1024,384]{1,0:T(8,128)(2,1)}, f32[1,384]{1,0:T(1,128)}, f32[1,384]{1,0:T(1,128)}) custom-call(s32[22]{0:T(128)} %pad_add_fusion.5.info_ref, bf16[6,1024,128]{2,1,0:T(8,128)(2,1)} %get-tuple-element.53.aug_ref, bf16[1024,384]{1,0:T(8,128)(2,1)} %get-tuple-element.43.k_ref, ...), custom_call_target="tpu_custom_call" | custom-call | flops 8053063680 | bytes 7864320 | tf_op jit(solution)/shard_map/attend_back/pallas_call | solution.py:358
  462.2 7.4 %fusion.11 = bf16[768,1152]{1,0:T(8,128)(2,1)} fusion(bf16[1024,1152]{1,0:T(8,128)(2,1)S(1)} %constant_dynamic-update-slice_fusion.3, bf16[1024,1152]{1,0:T(8,128)(2,1)S(1)} %copy-done.49, bf16[1024,768]{1,0:T(8,128)(2,1)} %get-tuple-element.59, bf16[1024,768]{1,0:T(8,128)(2,1)} %get-tuple-element.58), kind=kOutput, calls=%fused_computation.19 | convolution fusion | flops 3640492032 | bytes 9633792 | tf_op jit(solution)/shard_map/dot_general | solution.py:191
  481.2 6.0 reshape.870
  496.7 11.3 %collective-permute-done.37 = bf16[2,256,3,192]{1,3,2,0:T(8,128)(2,1)S(1)} collective-permute-done((bf16[2,256,3,192]{1,3,2,0:T(8,128)(2,1)S(1)}, bf16[2,256,3,192]{1,3,2,0:T(8,128)(2,1)S(1)}, u32[]{:S(2)}, u32[]{:S(2)}) %collective-permute-start.37) | collective-permute-done | bytes 589856 | tf_op jit(solution)/shard_map/ppermute | solution.py:36
  514.9 5.8 fusion.7
  578.0 6.4 collective-permute-done.43
  585.9 13.2 %collective-permute-start.81 = (bf16[96,768]{1,0:T(8,128)(2,1)S(1)}, bf16[96,768]{1,0:T(8,128)(2,1)S(1)}, u32[]{:S(2)}, u32[]{:S(2)}) collective-permute-start(bf16[96,768]{1,0:T(8,128)(2,1)S(1)} %get-tuple-element.160), channel_id=1, source_target_pairs={{0,2},{1,3},{2,0},{3,1},{4,6},{5,7},{6,4},{7,5},{8,10},{9,11},{10,... | collective-permute-start | bytes 442376 | tf_op jit(solution)/shard_map/ppermute | solution.py:36
  611.0 7.2 %collective-permute-done.70 = bf16[24,3072]{1,0:T(8,128)(2,1)S(1)} collective-permute-done((bf16[24,3072]{1,0:T(8,128)(2,1)S(1)}, bf16[24,3072]{1,0:T(8,128)(2,1)S(1)}, u32[]{:S(2)}, u32[]{:S(2)}) %collective-permute-start.70) | collective-permute-done | bytes 147488 | tf_op jit(solution)/shard_map/ppermute | solution.py:36
  629.2 6.9 %collective-permute-done.73 = bf16[24,3072]{1,0:T(8,128)(2,1)S(1)} collective-permute-done((bf16[24,3072]{1,0:T(8,128)(2,1)S(1)}, bf16[24,3072]{1,0:T(8,128)(2,1)S(1)}, u32[]{:S(2)}, u32[]{:S(2)}) %collective-permute-start.73) | collective-permute-done | bytes 147488 | tf_op jit(solution)/shard_map/ppermute | solution.py:36
  639.4 7.3 %collective-permute-done.84 = bf16[96,768]{1,0:T(8,128)(2,1)S(1)} collective-permute-done((bf16[96,768]{1,0:T(8,128)(2,1)S(1)}, bf16[96,768]{1,0:T(8,128)(2,1)S(1)}, u32[]{:S(2)}, u32[]{:S(2)}) %collective-permute-start.84) | collective-permute-done | bytes 147488 | tf_op jit(solution)/shard_map/ppermute | solution.py:36
  655.3 8.3 %collective-permute-done.48 = bf16[64,1152]{1,0:T(8,128)(2,1)S(1)} collective-permute-done((bf16[64,1152]{1,0:T(8,128)(2,1)S(1)}, bf16[64,1152]{1,0:T(8,128)(2,1)S(1)}, u32[]{:S(2)}, u32[]{:S(2)}) %collective-permute-start.48) | collective-permute-done | bytes 147488 | tf_op jit(solution)/shard_map/ppermute | solution.py:36
  670.4 8.4 %collective-permute-done.51 = bf16[64,1152]{1,0:T(8,128)(2,1)S(1)} collective-permute-done((bf16[64,1152]{1,0:T(8,128)(2,1)S(1)}, bf16[64,1152]{1,0:T(8,128)(2,1)S(1)}, u32[]{:S(2)}, u32[]{:S(2)}) %collective-permute-start.51) | collective-permute-done | bytes 147488 | tf_op jit(solution)/shard_map/ppermute | solution.py:36
  (645 shorter events, 311.6 us)
Async XLA Ops:
  2.7 49.8 %collective-permute-start.27 = (bf16[384,384]{1,0:T(8,128)(2,1)}, bf16[384,384]{1,0:T(8,128)(2,1)S(1)}, u32[]{:S(2)}, u32[]{:S(2)}) collective-permute-start(bf16[384,384]{1,0:T(8,128)(2,1)} %get-tuple-element.175), channel_id=1, source_target_pairs={{0,8},{8,0},{16,24},{24,16},{1,9},{9,1},{17,25},{25,17},{2,10},{10... | collective-permute-start | bytes 884744 | tf_op jit(solution)/shard_map/ppermute | solution.py:36
  5.7 48.5 %collective-permute-start.29 = (bf16[384,384]{1,0:T(8,128)(2,1)}, bf16[384,384]{1,0:T(8,128)(2,1)}, u32[]{:S(2)}, u32[]{:S(2)}) collective-permute-start(bf16[384,384]{1,0:T(8,128)(2,1)} %get-tuple-element.176), channel_id=1, source_target_pairs={{0,16},{8,24},{16,0},{24,8},{1,17},{9,25},{17,1},{25,9},{2,18},{10... | collective-permute-start | bytes 884744 | tf_op jit(solution)/shard_map/ppermute | solution.py:36
  9.1 39.7 %collective-permute-start.22 = (bf16[96,1536]{1,0:T(8,128)(2,1)}, bf16[96,1536]{1,0:T(8,128)(2,1)}, u32[]{:S(2)}, u32[]{:S(2)}) collective-permute-start(bf16[96,1536]{1,0:T(8,128)(2,1)} %get-tuple-element.179), channel_id=1, source_target_pairs={{0,8},{8,0},{16,24},{24,16},{1,9},{9,1},{17,25},{25,17},{2,10},{10... | collective-permute-start | bytes 884744 | tf_op jit(solution)/shard_map/ppermute | solution.py:36
  47.9 27.6 %collective-permute-start.2 = (bf16[256,768]{1,0:T(8,128)(2,1)S(1)}, bf16[256,768]{1,0:T(8,128)(2,1)S(1)}, u32[]{:S(2)}, u32[]{:S(2)}) collective-permute-start(bf16[256,768]{1,0:T(8,128)(2,1)S(1)} %copy-done.46), channel_id=1, source_target_pairs={{0,0},{1,1},{2,4},{3,5},{4,2},{5,3},{6,6},{7,7},{8,8},{9,9},{10,12... | collective-permute-start | bytes 1179656 | tf_op jit(solution)/shard_map/ppermute | solution.py:514
  61.9 49.1 %collective-permute-start.18 = (bf16[4,96,768]{2,1,0:T(8,128)(2,1)S(1)}, bf16[4,96,768]{2,1,0:T(8,128)(2,1)S(1)}, u32[]{:S(2)}, u32[]{:S(2)}) collective-permute-start(bf16[4,96,768]{2,1,0:T(8,128)(2,1)S(1)} %pad_maximum_fusion.27), channel_id=1, source_target_pairs={{0,4},{4,0},{1,5},{5,1},{2,6},{6,2},{3,7},{7,3},{8,12},{12,8},{9,1... | collective-permute-start | bytes 1769480 | tf_op jit(solution)/shard_map/ppermute | solution.py:36
  76.8 25.2 %collective-permute-start.8 = (bf16[224,640]{1,0:T(8,128)(2,1)S(1)}, bf16[224,640]{1,0:T(8,128)(2,1)S(1)}, u32[]{:S(2)}, u32[]{:S(2)}) collective-permute-start(bf16[224,640]{1,0:T(8,128)(2,1)S(1)} %slice.215), channel_id=1, source_target_pairs={{0,16},{8,24},{16,0},{24,8},{1,17},{9,25},{17,1},{25,9},{2,18},{10... | collective-permute-start | bytes 860168 | tf_op jit(solution)/shard_map/ppermute | solution.py:36
  78.4 40.3 %collective-permute-start.28 = (bf16[2,384,384]{2,1,0:T(8,128)(2,1)S(1)}, bf16[2,384,384]{2,1,0:T(8,128)(2,1)S(1)}, u32[]{:S(2)}, u32[]{:S(2)}) collective-permute-start(bf16[2,384,384]{2,1,0:T(8,128)(2,1)S(1)} %pad_maximum_fusion.30), channel_id=1, source_target_pairs={{0,16},{8,24},{16,0},{24,8},{1,17},{9,25},{17,1},{25,9},{2,18},{10... | collective-permute-start | bytes 1769480 | tf_op jit(solution)/shard_map/ppermute | solution.py:36
  79.0 41.5 %collective-permute-start.30 = (bf16[2,384,384]{2,1,0:T(8,128)(2,1)S(1)}, bf16[2,384,384]{2,1,0:T(8,128)(2,1)S(1)}, u32[]{:S(2)}, u32[]{:S(2)}) collective-permute-start(bf16[2,384,384]{2,1,0:T(8,128)(2,1)S(1)} %pad_maximum_fusion.31), channel_id=1, source_target_pairs={{0,8},{8,0},{16,24},{24,16},{1,9},{9,1},{17,25},{25,17},{2,10},{10... | collective-permute-start | bytes 1769480 | tf_op jit(solution)/shard_map/ppermute | solution.py:36
  83.3 25.4 %collective-permute-start.10 = (bf16[256,768]{1,0:T(8,128)(2,1)S(1)}, bf16[256,768]{1,0:T(8,128)(2,1)S(1)}, u32[]{:S(2)}, u32[]{:S(2)}) collective-permute-start(bf16[256,768]{1,0:T(8,128)(2,1)S(1)} %collective-permute-done.2), channel_id=1, source_target_pairs={{0,1},{1,0},{2,3},{3,2},{4,5},{5,4},{6,7},{7,6},{8,9},{9,8},{10,11... | collective-permute-start | bytes 1179656 | tf_op jit(solution)/shard_map/ppermute | solution.py:36
  111.0 29.7 %collective-permute-start.4 = (bf16[512,768]{1,0:T(8,128)(2,1)}, bf16[512,768]{1,0:T(8,128)(2,1)}, u32[]{:S(2)}, u32[]{:S(2)}) collective-permute-start(bf16[512,768]{1,0:T(8,128)(2,1)} %pad_maximum_fusion.20), channel_id=1, source_target_pairs={{0,4},{4,0},{1,5},{5,1},{2,6},{6,2},{3,7},{7,3},{8,12},{12,8},{9,1... | collective-permute-start | bytes 2359304 | tf_op jit(solution)/shard_map/ppermute | solution.py:36
  123.6 136.9 %collective-permute-start.31 = (bf16[4,384,768]{2,1,0:T(8,128)(2,1)}, bf16[4,384,768]{2,1,0:T(8,128)(2,1)}, u32[]{:S(2)}, u32[]{:S(2)}) collective-permute-start(bf16[4,384,768]{2,1,0:T(8,128)(2,1)} %pad_maximum_fusion.3), channel_id=1, source_target_pairs={{0,4},{4,0},{1,5},{5,1},{2,6},{6,2},{3,7},{7,3},{8,12},{12,8},{9,1... | collective-permute-start | bytes 7077896 | tf_op jit(solution)/shard_map/ppermute | solution.py:36
  192.9 51.6 %collective-permute-start.12 = (bf16[2,256,192]{1,2,0:T(8,128)(2,1)S(1)}, bf16[2,256,192]{1,2,0:T(8,128)(2,1)S(1)}, u32[]{:S(2)}, u32[]{:S(2)}) collective-permute-start(bf16[2,256,192]{1,2,0:T(8,128)(2,1)S(1)} %bitcast.565), channel_id=1, source_target_pairs={{0,1},{1,0},{2,3},{3,2},{4,5},{5,4},{6,7},{7,6},{8,9},{9,8},{10,11... | collective-permute-start | bytes 589832 | tf_op jit(solution)/shard_map/ppermute | solution.py:36
  315.7 209.7 %collective-permute-start.75 = (bf16[4,384,768]{2,1,0:T(8,128)(2,1)}, bf16[4,384,768]{2,1,0:T(8,128)(2,1)}, u32[]{:S(2)}, u32[]{:S(2)}) collective-permute-start(bf16[4,384,768]{2,1,0:T(8,128)(2,1)} %dynamic-slice_bitcast_fusion), channel_id=1, source_target_pairs={{0,4},{4,0},{1,5},{5,1},{2,6},{6,2},{3,7},{7,3},{8,12},{12,8},{9,1... | collective-permute-start | bytes 7077896 | tf_op jit(solution)/shard_map/ppermute | solution.py:36
  330.7 203.9 %collective-permute-start.64 = (bf16[4,96,3072]{2,1,0:T(8,128)(2,1)}, bf16[4,96,3072]{2,1,0:T(8,128)(2,1)}, u32[]{:S(2)}, u32[]{:S(2)}) collective-permute-start(bf16[4,96,3072]{2,1,0:T(8,128)(2,1)} %dynamic-slice_bitcast_fusion.1), channel_id=1, source_target_pairs={{0,4},{4,0},{1,5},{5,1},{2,6},{6,2},{3,7},{7,3},{8,12},{12,8},{9,1... | collective-permute-start | bytes 7077896 | tf_op jit(solution)/shard_map/ppermute | solution.py:36
  342.8 70.6 %collective-permute-start.54 = (bf16[2,96,384]{2,1,0:T(8,128)(2,1)}, bf16[2,96,384]{2,1,0:T(8,128)(2,1)}, u32[]{:S(2)}, u32[]{:S(2)}) collective-permute-start(bf16[2,96,384]{2,1,0:T(8,128)(2,1)} %dynamic-slice_bitcast_fusion.31), channel_id=1, source_target_pairs={{0,8},{8,0},{16,24},{24,16},{1,9},{9,1},{17,25},{25,17},{2,10},{10... | collective-permute-start | bytes 442376 | tf_op jit(solution)/shard_map/ppermute | solution.py:36
  342.9 72.3 %collective-permute-start.56 = (bf16[2,96,384]{2,1,0:T(8,128)(2,1)S(1)}, bf16[2,96,384]{2,1,0:T(8,128)(2,1)}, u32[]{:S(2)}, u32[]{:S(2)}) collective-permute-start(bf16[2,96,384]{2,1,0:T(8,128)(2,1)S(1)} %dynamic-slice_bitcast_fusion.30), channel_id=1, source_target_pairs={{0,16},{8,24},{16,0},{24,8},{1,17},{9,25},{17,1},{25,9},{2,18},{10... | collective-permute-start | bytes 442376 | tf_op jit(solution)/shard_map/ppermute | solution.py:36
  415.1 54.7 %collective-permute-start.55 = (bf16[96,384]{1,0:T(8,128)(2,1)}, bf16[96,384]{1,0:T(8,128)(2,1)}, u32[]{:S(2)}, u32[]{:S(2)}) collective-permute-start(bf16[96,384]{1,0:T(8,128)(2,1)} %dynamic-slice_bitcast_fusion.36), channel_id=1, source_target_pairs={{0,16},{8,24},{16,0},{24,8},{1,17},{9,25},{17,1},{25,9},{2,18},{10... | collective-permute-start | bytes 221192 | tf_op jit(solution)/shard_map/ppermute | solution.py:36
  416.8 54.0 %collective-permute-start.57 = (bf16[96,384]{1,0:T(8,128)(2,1)}, bf16[96,384]{1,0:T(8,128)(2,1)}, u32[]{:S(2)}, u32[]{:S(2)}) collective-permute-start(bf16[96,384]{1,0:T(8,128)(2,1)} %dynamic-slice_bitcast_fusion.35), channel_id=1, source_target_pairs={{0,8},{8,0},{16,24},{24,16},{1,9},{9,1},{17,25},{25,17},{2,10},{10... | collective-permute-start | bytes 221192 | tf_op jit(solution)/shard_map/ppermute | solution.py:36
  546.6 30.8 %collective-permute-start.42 = (bf16[2,208,512]{2,1,0:T(8,128)(2,1)S(1)}, bf16[2,208,512]{2,1,0:T(8,128)(2,1)S(1)}, u32[]{:S(2)}, u32[]{:S(2)}) collective-permute-start(bf16[2,208,512]{2,1,0:T(8,128)(2,1)S(1)} %dynamic-slice_bitcast_fusion.10), channel_id=1, source_target_pairs={{0,8},{8,0},{16,24},{24,16},{1,9},{9,1},{17,25},{25,17},{2,10},{10... | collective-permute-start | bytes 1277960 | tf_op jit(solution)/shard_map/ppermute | solution.py:36
  551.0 26.8 %collective-permute-start.44 = (bf16[2,208,640]{2,1,0:T(8,128)(2,1)S(1)}, bf16[2,208,640]{2,1,0:T(8,128)(2,1)S(1)}, u32[]{:S(2)}, u32[]{:S(2)}) collective-permute-start(bf16[2,208,640]{2,1,0:T(8,128)(2,1)S(1)} %dynamic-slice_bitcast_fusion.9), channel_id=1, source_target_pairs={{0,16},{8,24},{16,0},{24,8},{1,17},{9,25},{17,1},{25,9},{2,18},{10... | collective-permute-start | bytes 1597448 | tf_op jit(solution)/shard_map/ppermute | solution.py:36
  571.6 27.6 %collective-permute-start.66 = (bf16[96,1536]{1,0:T(8,128)(2,1)S(1)}, bf16[96,1536]{1,0:T(8,128)(2,1)S(1)}, u32[]{:S(2)}, u32[]{:S(2)}) collective-permute-start(bf16[96,1536]{1,0:T(8,128)(2,1)S(1)} %dynamic-slice_bitcast_fusion.20), channel_id=1, source_target_pairs={{0,16},{8,24},{16,0},{24,8},{1,17},{9,25},{17,1},{25,9},{2,18},{10... | collective-permute-start | bytes 884744 | tf_op jit(solution)/shard_map/ppermute | solution.py:36
  585.9 36.2 %collective-permute-start.80 = (bf16[96,768]{1,0:T(8,128)(2,1)S(1)}, bf16[96,768]{1,0:T(8,128)(2,1)S(1)}, u32[]{:S(2)}, u32[]{:S(2)}) collective-permute-start(bf16[96,768]{1,0:T(8,128)(2,1)S(1)} %get-tuple-element.158), channel_id=1, source_target_pairs={{0,1},{1,0},{2,3},{3,2},{4,5},{5,4},{6,7},{7,6},{8,9},{9,8},{10,11... | collective-permute-start | bytes 442376 | tf_op jit(solution)/shard_map/ppermute | solution.py:36
  585.9 36.5 %collective-permute-start.81 = (bf16[96,768]{1,0:T(8,128)(2,1)S(1)}, bf16[96,768]{1,0:T(8,128)(2,1)S(1)}, u32[]{:S(2)}, u32[]{:S(2)}) collective-permute-start(bf16[96,768]{1,0:T(8,128)(2,1)S(1)} %get-tuple-element.160), channel_id=1, source_target_pairs={{0,2},{1,3},{2,0},{3,1},{4,6},{5,7},{6,4},{7,5},{8,10},{9,11},{10,... | collective-permute-start | bytes 442376 | tf_op jit(solution)/shard_map/ppermute | solution.py:36
  618.2 28.7 %collective-permute-start.46 = (bf16[112,1152]{1,0:T(8,128)(2,1)S(1)}, bf16[112,1152]{1,0:T(8,128)(2,1)S(1)}, u32[]{:S(2)}, u32[]{:S(2)}) collective-permute-start(bf16[112,1152]{1,0:T(8,128)(2,1)S(1)} %pad_maximum_fusion.44), channel_id=1, source_target_pairs={{0,4},{4,0},{1,5},{5,1},{2,6},{6,2},{3,7},{7,3},{8,12},{12,8},{9,1... | collective-permute-start | bytes 774152 | tf_op jit(solution)/shard_map/ppermute | solution.py:36
  (142 other events, 1577.9 us)

commit v2 on v1

v2 whole, which is shorter than its diff:
```python
import functools

import jax
import jax.numpy as jnp
from jax import lax
from jax.experimental import pallas as pl
from jax.experimental.pallas import tpu as pltpu
from jax.sharding import Mesh, PartitionSpec as P

HEADS = 12
HEAD = 64
EPSILON = 1e-06
BLOCK = 256
STEP = 512
MARK = 32.0
EXP2_FACTOR = HEAD**-0.5 * 1.4426950408889634
F32 = jnp.float32
BF16 = jnp.bfloat16
VMEM_LIMIT = 56 * 1024 * 1024

SEQ = ("zp", "zq")
COLUMN = ("core", "zp", "zq")
KEEP = [
    (core * 4 + z, (z // 2) * 4 + 2 * core + z % 2) for core in range(2) for z in range(4)
]
CROSS = [
    (core * 4 + z, (z // 2) * 4 + 2 * core + 1 - z % 2) for core in range(2) for z in range(4)
]


def swap(array, name, bit=1):
    count = lax.axis_size(name)
    return lax.ppermute(array, name, [(i, i ^ bit) for i in range(count)])


def pick(array, index, axis=0):
    return lax.dynamic_index_in_dim(array, index, axis, keepdims=False)


def group_ones(scale):
    row = lax.broadcasted_iota(jnp.int32, (128, 128), 0) // HEAD
    column = lax.broadcasted_iota(jnp.int32, (128, 128), 1) // HEAD
    return jnp.where(row == column, scale, 0.0).astype(BF16)


def group_sum(values, ones):
    high = values.astype(BF16)
    low = (values - high.astype(F32)).astype(BF16)
    return jnp.dot(high, ones, preferred_element_type=F32) + jnp.dot(
        low, ones, preferred_element_type=F32
    )


def project_kernel(x_ref, gain_ref, weight_ref, qg_ref, kg_ref, normed_ref, q_ref, k_ref, v_ref, raw_ref):
    width = q_ref.shape[1]
    x = x_ref[...].astype(F32)
    center = x - jnp.mean(x, axis=-1, keepdims=True)
    spread = jnp.mean(center * center, axis=-1, keepdims=True)
    normed = (center * lax.rsqrt(spread + EPSILON) * gain_ref[...]).astype(BF16)
    normed_ref[...] = normed
    mixed = jnp.dot(normed, weight_ref[...], preferred_element_type=F32)
    raw_ref[...] = mixed[:, : 2 * width]
    ones = group_ones(1.0 / HEAD)
    for part, (out_ref, g_ref) in enumerate(((q_ref, qg_ref), (k_ref, kg_ref))):
        for at in range(0, width, 128):
            raw = mixed[:, part * width + at : part * width + at + 128]
            c = raw - group_sum(raw, ones)
            n = c * lax.rsqrt(group_sum(c * c, ones) + EPSILON)
            out_ref[:, at : at + 128] = (n * g_ref[:, at : at + 128]).astype(BF16)
    v_ref[...] = mixed[:, 2 * width :].astype(BF16)


def project(x, gain, weight, query_gain, key_gain):
    tokens, model = x.shape
    width = weight.shape[1] // 3
    whole = lambda shape: pl.BlockSpec(shape, lambda i: (0, 0))
    rows = lambda columns: pl.BlockSpec((BLOCK, columns), lambda i: (i, 0))
    return pl.pallas_call(
        project_kernel,
        grid=(tokens // BLOCK,),
        in_specs=[
            rows(model),
            whole((1, model)),
            whole(weight.shape),
            whole((1, width)),
            whole((1, width)),
        ],
        out_specs=[rows(model), rows(width), rows(width), rows(width), rows(2 * width)],
        out_shape=[
            jax.ShapeDtypeStruct((tokens, model), BF16),
            jax.ShapeDtypeStruct((tokens, width), BF16),
            jax.ShapeDtypeStruct((tokens, width), BF16),
            jax.ShapeDtypeStruct((tokens, width), BF16),
            jax.ShapeDtypeStruct((tokens, 2 * width), F32),
        ],
        compiler_params=pltpu.CompilerParams(vmem_limit_bytes=VMEM_LIMIT),
        cost_estimate=pl.CostEstimate(
            flops=2 * tokens * model * 3 * width, bytes_accessed=tokens * model * 12, transcendentals=0
        ),
        name="project",
    )(x, gain, weight, query_gain, key_gain)


def nt(a, b):
    return lax.dot_general(a, b, (((1,), (1,)), ((), ())), preferred_element_type=F32)


def tn(a, b):
    return lax.dot_general(a, b, (((0,), (0,)), ((), ())), preferred_element_type=F32)


def slots(queries, length, part):
    at = lax.broadcasted_iota(jnp.int32, (queries, 128), 0)
    if queries == length:
        return at
    return at % part + part * (lax.axis_index("zq") + 2 * (at // part))


def own_rows(ref, start, count, queries, part):
    if queries == ref.shape[0]:
        return ref[pl.ds(start, count), :]
    zq = lax.axis_index("zq")
    pieces = [
        ref[pl.ds(pl.multiple_of((zq + 2 * i) * part, part), part), :]
        for i in range(start // part, (start + count) // part)
    ]
    return jnp.concatenate(pieces, axis=0)


def query_marks(bounds_ref, place, queries, length, part, pics):
    at = slots(queries, length, part)
    inside = (at >= bounds_ref[0:1, :]) & (at < bounds_ref[2:3, :])
    values = jnp.where(inside, MARK, 0.0)
    return jnp.where(place == pics, MARK, values).astype(BF16)


def key_marks(bounds_ref, place, length, pics):
    at = lax.broadcasted_iota(jnp.int32, (length, 128), 0)
    inside = (at >= bounds_ref[0:1, :]) & (at < bounds_ref[1:2, :])
    values = jnp.where(inside, MARK, 0.0)
    values = jnp.where(place == pics, -MARK, values)
    return jnp.where((place > pics) & (place < pics + 4), 1.0, values).astype(BF16)


def attend_kernel(pics, q_ref, k_ref, v_ref, bounds_ref, out_ref, aug_ref, kaug, vaug, qaug):
    length = k_ref.shape[0]
    queries = out_ref.shape[0]
    part = length // 4
    lane = lax.broadcasted_iota(jnp.int32, (1, 128), 1)
    place = lane % HEAD
    sides = [lane < HEAD, lane >= HEAD]
    kmarks = key_marks(bounds_ref, place, length, pics)
    qmarks = query_marks(bounds_ref, place, queries, length, part, pics)
    qaug[...] = qmarks
    for h in range(2):
        kaug[h] = jnp.where(sides[h], k_ref[...], kmarks)
        vaug[h] = jnp.where(sides[h], v_ref[...], jnp.ones_like(v_ref))
    for b in range(queries // STEP):
        rows = pl.ds(b * STEP, STEP)
        mine = own_rows(q_ref, b * STEP, STEP, queries, part)
        query = [jnp.where(sides[h], mine, qaug[rows, :]) for h in range(2)]
        total = [jnp.zeros((STEP, 128), F32)] * 2
        for j in range(length // STEP):
            keys = pl.ds(j * STEP, STEP)
            scores = [nt(query[h], kaug[h, keys, :]) for h in range(2)]
            weights = [jnp.exp2(x * EXP2_FACTOR).astype(BF16) for x in scores]
            total = [
                total[h] + jnp.dot(weights[h], vaug[h, keys, :], preferred_element_type=F32) for h in range(2)
            ]
        results = []
        for h in range(2):
            results.append(total[h] / pltpu.roll(total[h], HEAD, 1))
            log_total = jnp.log(jnp.where(sides[h], 1.0, total[h])) * -(HEAD**0.5)
            first = log_total.astype(BF16)
            rest = log_total - first.astype(F32)
            middle = rest.astype(BF16)
            last = (rest - middle.astype(F32)).astype(BF16)
            logs = jnp.where(place == pics + 1, first, jnp.where(place == pics + 2, middle, last))
            slot = jnp.logical_not(sides[h]) & (place > pics) & (place < pics + 4)
            aug_ref[h, rows, :] = jnp.where(slot, logs, query[h])
        out_ref[rows, :] = jnp.where(sides[0], results[0], results[1]).astype(BF16)


def attend(q, k, v, bounds, pics, queries):
    length, width = k.shape
    pairs = width // 128
    column = pl.BlockSpec((length, 128), lambda p: (0, p))
    return pl.pallas_call(
        functools.partial(attend_kernel, pics),
        grid=(pairs,),
        in_specs=[column, column, column, pl.BlockSpec((8, 128), lambda p: (0, 0))],
        out_specs=[
            pl.BlockSpec((queries, 128), lambda p: (0, p)),
            pl.BlockSpec((2, queries, 128), lambda p: (p, 0, 0)),
        ],
        scratch_shapes=[
            pltpu.VMEM((2, length, 128), BF16),
            pltpu.VMEM((2, length, 128), BF16),
            pltpu.VMEM((queries, 128), BF16),
        ],
        out_shape=[
            jax.ShapeDtypeStruct((queries, width), BF16),
            jax.ShapeDtypeStruct((2 * pairs, queries, 128), BF16),
        ],
        compiler_params=pltpu.CompilerParams(vmem_limit_bytes=VMEM_LIMIT),
        cost_estimate=pl.CostEstimate(
            flops=16 * length * queries * width, bytes_accessed=length * width * 12, transcendentals=0
        ),
        name="attend",
    )(q, k, v, bounds)


def head_norm_back(e, raw, gain, means):
    c = raw - group_sum(raw, means)
    r = lax.rsqrt(group_sum(c * c, means) + EPSILON)
    n = c * r
    t = e * gain
    grad = r * (t - group_sum(t, means) - n * group_sum(t * n, means))
    return grad.astype(BF16), jnp.sum(e * n, axis=0, keepdims=True)


def attend_back_kernel(
    pics, aug_ref, k_ref, v_ref, out_ref, do_ref, rawq_ref, rawk_ref, qg_ref, kg_ref, bounds_ref,
    dq_ref, dk_ref, dv_ref, qgg_ref, kgg_ref, kaug, vaug, doaug, qsum, ksum,
):
    length = k_ref.shape[0]
    queries = do_ref.shape[0]
    part = length // 4
    whole = queries == length
    lane = lax.broadcasted_iota(jnp.int32, (1, 128), 1)
    place = lane % HEAD
    sides = [lane < HEAD, lane >= HEAD]
    kmarks = key_marks(bounds_ref, place, length, pics)
    vmarks = jnp.where(place < 2, 1.0, 0.0).astype(BF16)
    ones = group_ones(1.0)
    inner = group_sum(do_ref[...].astype(F32) * out_ref[...].astype(F32), ones)
    inner = -pltpu.roll(inner, HEAD, 1)
    inner_high = inner.astype(BF16)
    inner_low = (inner - inner_high.astype(F32)).astype(BF16)
    zero = jnp.zeros((), BF16)
    gmarks = jnp.where(place == 0, inner_high, jnp.where(place == 1, inner_low, zero))
    for h in range(2):
        kaug[h] = jnp.where(sides[h], k_ref[...], kmarks)
        vaug[h] = jnp.where(sides[h], v_ref[...], vmarks)
        doaug[h] = jnp.where(sides[h], do_ref[...], gmarks)
    for b in range(length // STEP):
        keys = pl.ds(b * STEP, STEP)
        key = [kaug[h, keys, :] for h in range(2)]
        value = [vaug[h, keys, :] for h in range(2)]
        dk = [jnp.zeros((STEP, 128), F32)] * 2
        dv = [jnp.zeros((STEP, 128), F32)] * 2
        for j in range(queries // STEP):
            rows = pl.ds(j * STEP, STEP)
            query = [aug_ref[h, rows, :] for h in range(2)]
            grad = [doaug[h, rows, :] for h in range(2)]
            scores = [nt(key[h], query[h]) for h in range(2)]
            soft_grad = [nt(value[h], grad[h]) for h in range(2)]
            weights = [jnp.exp2(x * EXP2_FACTOR) for x in scores]
            score_grad = [(weights[h] * soft_grad[h]).astype(BF16) for h in range(2)]
            for h in range(2):
                part_sum = tn(score_grad[h], key[h])
                if b == 0:
                    qsum[h, rows, :] = part_sum
                else:
                    qsum[h, rows, :] += part_sum
                dk[h] = dk[h] + jnp.dot(score_grad[h], query[h], preferred_element_type=F32)
                dv[h] = dv[h] + jnp.dot(weights[h].astype(BF16), grad[h], preferred_element_type=F32)
        ksum[keys, :] = jnp.where(sides[0], dk[0], dk[1]) * HEAD**-0.5
        dv_ref[keys, :] = jnp.where(sides[0], dv[0], dv[1]).astype(BF16)

    means = group_ones(1.0 / HEAD)
    gain_sum = jnp.zeros((1, 128), F32)
    for b in range(queries // part):
        rows = pl.ds(b * part, part)
        e = jnp.where(sides[0], qsum[0, rows, :], qsum[1, rows, :]) * HEAD**-0.5
        raw = own_rows(rawq_ref, b * part, part, queries, part)
        dq_ref[rows, :], more = head_norm_back(e.astype(BF16).astype(F32), raw, qg_ref[...], means)
        gain_sum = gain_sum + more
    qgg_ref[...] = gain_sum
    gain_sum = jnp.zeros((1, 128), F32)
    for b in range(length // part):
        rows = pl.ds(b * part, part)
        e = ksum[rows, :].astype(BF16)
        if whole:
            dk_ref[rows, :], more = head_norm_back(e.astype(F32), rawk_ref[rows, :], kg_ref[...], means)
            gain_sum = gain_sum + more
        else:
            dk_ref[rows, :] = e
    kgg_ref[...] = gain_sum


def attend_back(aug, k, v, out, do, raw, query_gain, key_gain, bounds, pics):
    length, width = k.shape
    queries = do.shape[0]
    pairs = width // 128
    column = pl.BlockSpec((length, 128), lambda p: (0, p))
    own = pl.BlockSpec((queries, 128), lambda p: (0, p))
    gain = pl.BlockSpec((1, 128), lambda p: (0, p))
    return pl.pallas_call(
        functools.partial(attend_back_kernel, pics),
        grid=(pairs,),
        in_specs=[
            pl.BlockSpec((2, queries, 128), lambda p: (p, 0, 0)),
            column,
            column,
            own,
            own,
            column,
            pl.BlockSpec((length, 128), lambda p: (0, pairs + p)),
            gain,
            gain,
            pl.BlockSpec((8, 128), lambda p: (0, 0)),
        ],
        out_specs=[own, column, column, gain, gain],
        scratch_shapes=[
            pltpu.VMEM((2, length, 128), BF16),
            pltpu.VMEM((2, length, 128), BF16),
            pltpu.VMEM((2, queries, 128), BF16),
            pltpu.VMEM((2, queries, 128), F32),
            pltpu.VMEM((length, 128), F32),
        ],
        out_shape=[
            jax.ShapeDtypeStruct((queries, width), BF16),
            jax.ShapeDtypeStruct((length, width), BF16),
            jax.ShapeDtypeStruct((length, width), BF16),
            jax.ShapeDtypeStruct((1, width), F32),
            jax.ShapeDtypeStruct((1, width), F32),
        ],
        compiler_params=pltpu.CompilerParams(vmem_limit_bytes=VMEM_LIMIT),
        cost_estimate=pl.CostEstimate(
            flops=40 * length * queries * width, bytes_accessed=length * width * 20, transcendentals=0
        ),
        name="attend_back",
    )(aug, k, v, out, do, raw, raw, query_gain, key_gain, bounds)


def shared_keys_kernel(dk_ref, dv_ref, gotk_ref, gotv_ref, rawk_ref, kg_ref, outk_ref, outv_ref, kgg_ref):
    count = outk_ref.shape[0]
    part = count // 2
    means = group_ones(1.0 / HEAD)
    gain_sum = jnp.zeros((1, 128), F32)
    for b in range(2):
        rows = pl.ds(b * part, part)
        own = lambda ref: own_rows(ref, b * part, part, count, part)
        e = own(dk_ref).astype(F32) + gotk_ref[rows, :].astype(F32)
        outk_ref[rows, :], more = head_norm_back(e, own(rawk_ref), kg_ref[...], means)
        gain_sum = gain_sum + more
        outv_ref[rows, :] = (own(dv_ref).astype(F32) + gotv_ref[rows, :].astype(F32)).astype(BF16)
    kgg_ref[...] = gain_sum


def shared_keys(dk, dv, got_k, got_v, raw, key_gain):
    length, width = dk.shape
    pairs = width // 128
    column = pl.BlockSpec((length, 128), lambda p: (0, p))
    own = pl.BlockSpec((length // 2, 128), lambda p: (0, p))
    gain = pl.BlockSpec((1, 128), lambda p: (0, p))
    return pl.pallas_call(
        shared_keys_kernel,
        grid=(pairs,),
        in_specs=[column, column, own, own, pl.BlockSpec((length, 128), lambda p: (0, pairs + p)), gain],
        out_specs=[own, own, gain],
        out_shape=[
            jax.ShapeDtypeStruct((length // 2, width), BF16),
            jax.ShapeDtypeStruct((length // 2, width), BF16),
            jax.ShapeDtypeStruct((1, width), F32),
        ],
        compiler_params=pltpu.CompilerParams(vmem_limit_bytes=VMEM_LIMIT),
        name="shared_keys",
    )(dk, dv, got_k, got_v, raw, key_gain)


def gelu_pair(h):
    size = jnp.abs(h)
    bell = jnp.exp2(h * h * -0.7213475204444817)
    t = 1.0 / (1.0 + 0.23164189 * size)
    series = t * (0.127414796 + t * (-0.142248368 + t * (0.7107068705 + t * (-0.7265760135 + t * 0.5307027145))))
    tail = series * bell
    below = jnp.where(h < 0.0, tail, 1.0 - tail)
    return h * below, below + h * (bell * 0.3989422804014327)


def norm_parts(values):
    center = values - jnp.mean(values, axis=-1, keepdims=True)
    spread = lax.rsqrt(jnp.mean(center * center, axis=-1, keepdims=True) + EPSILON)
    return center * spread, spread


def norm_back(upstream, n, r, gain):
    t = upstream * gain
    grad = r * (t - jnp.mean(t, axis=-1, keepdims=True) - n * jnp.mean(t * n, axis=-1, keepdims=True))
    return grad, jnp.sum(upstream * n, axis=0, keepdims=True)


def dense_kernel(
    attended_ref, x_ref, outw_ref, gain_ref, grad_ref, up_ref, down_ref,
    output_ref, midg_ref, attg_ref, outg_ref, upg_ref, downg_ref, gaing_ref,
    middle, second, forward, backward,
):
    step = pl.program_id(0)
    tokens = x_ref.shape[0]
    blocks = [pl.ds(b * BLOCK, BLOCK) for b in range(tokens // BLOCK)]

    @pl.when(step == 0)
    def _():
        for rows in blocks:
            value = x_ref[rows, :].astype(F32) + jnp.dot(
                attended_ref[rows, :], outw_ref[...], preferred_element_type=F32
            )
            middle[rows, :] = value
            second[rows, :] = (norm_parts(value)[0] * gain_ref[...]).astype(BF16)
        forward[...] = jnp.zeros_like(forward)
        backward[...] = jnp.zeros_like(backward)

    up = up_ref[...]
    down = down_ref[...]
    pre = jnp.dot(second[...], up, preferred_element_type=F32)
    hidden, slope = gelu_pair(pre)
    hidden = hidden.astype(BF16)
    forward[...] += jnp.dot(hidden, down, preferred_element_type=F32)
    pre_grad = (nt(grad_ref[...], down) * slope).astype(BF16)
    downg_ref[...] = tn(hidden, grad_ref[...]).astype(BF16)
    upg_ref[...] = tn(second[...], pre_grad).astype(BF16)
    backward[...] += nt(pre_grad, up)

    @pl.when(step == pl.num_programs(0) - 1)
    def _():
        gain_sum = jnp.zeros(gaing_ref.shape, F32)
        for rows in blocks:
            value = middle[rows, :]
            output_ref[rows, :] = (value + forward[rows, :]).astype(BF16)
            n, r = norm_parts(value)
            part, more = norm_back(backward[rows, :], n, r, gain_ref[...])
            gain_sum = gain_sum + more
            value = grad_ref[rows, :].astype(F32) + part
            midg_ref[rows, :] = value
            branch = value.astype(BF16)
            second[rows, :] = branch
            attg_ref[rows, :] = nt(branch, outw_ref[...]).astype(BF16)
        gaing_ref[...] = gain_sum
        outg_ref[...] = tn(attended_ref[...], second[...]).astype(BF16)


def dense(attended, x, out_matrix, gain, grad, up, down):
    tokens, model = x.shape
    hidden = up.shape[1]
    tile = 512
    whole = pl.BlockSpec((tokens, model), lambda i: (0, 0))
    square = pl.BlockSpec((model, model), lambda i: (0, 0))
    line = pl.BlockSpec((1, model), lambda i: (0, 0))
    wide = pl.BlockSpec((model, tile), lambda i: (0, i))
    tall = pl.BlockSpec((tile, model), lambda i: (i, 0))
    return pl.pallas_call(
        dense_kernel,
        grid=(hidden // tile,),
        in_specs=[whole, whole, square, line, whole, wide, tall],
        out_specs=[whole, whole, whole, square, wide, tall, line],
        out_shape=[
            jax.ShapeDtypeStruct((tokens, model), BF16),
            jax.ShapeDtypeStruct((tokens, model), F32),
            jax.ShapeDtypeStruct((tokens, model), BF16),
            jax.ShapeDtypeStruct((model, model), BF16),
            jax.ShapeDtypeStruct((model, hidden), BF16),
            jax.ShapeDtypeStruct((hidden, model), BF16),
            jax.ShapeDtypeStruct((1, model), F32),
        ],
        scratch_shapes=[
            pltpu.VMEM((tokens, model), F32),
            pltpu.VMEM((tokens, model), BF16),
            pltpu.VMEM((tokens, model), F32),
            pltpu.VMEM((tokens, model), F32),
        ],
        compiler_params=pltpu.CompilerParams(vmem_limit_bytes=VMEM_LIMIT),
        cost_estimate=pl.CostEstimate(
            flops=16 * tokens * model * hidden, bytes_accessed=8 * model * hidden, transcendentals=0
        ),
        name="dense",
    )(attended, x, out_matrix, gain, grad, up, down)


MESH_ID = pl.DeviceIdType.MESH


def here():
    return lax.axis_index("chip"), lax.axis_index("core"), lax.axis_index("zp"), lax.axis_index("zq")


def remote(source, target, sems, at, device):
    sent, got = sems
    return pltpu.make_async_remote_copy(
        src_ref=source, dst_ref=target, send_sem=sent.at[at], recv_sem=got.at[at],
        device_id=device, device_id_type=MESH_ID,
    )


def greet(devices, maybe=None, moves=None):
    barrier = pltpu.get_barrier_semaphore()
    for device in devices:
        pl.semaphore_signal(barrier, inc=1, device_id=device, device_id_type=MESH_ID)
    if maybe is None:
        pl.semaphore_wait(barrier, len(devices))
        return

    @pl.when(moves)
    def _():
        pl.semaphore_signal(barrier, inc=1, device_id=maybe, device_id_type=MESH_ID)

    pl.semaphore_wait(barrier, len(devices) + jnp.where(moves, 1, 0))


def rows_at(start, count):
    return pl.ds(pl.multiple_of(start, 16), count)


def gather_kernel(
    with_mix, tokens_ref, lens_ref, mix_ref, gains_ref,
    row_ref, shared_ref, lens_out, mix_out, gains_out, sent, got, local_sem,
):
    chip, core, zp, zq = here()
    z = 2 * zp + zq
    part = tokens_ref.shape[1]
    sems = (sent, got)
    partner = (chip, 1 - core, zp, zq)
    side = (chip, core, zp, 1 - zq)
    keep = (chip, zp, core, zq)
    cross = (chip, zp, core, 1 - zq)
    moves = core != zp
    near_x = (chip ^ 1, core, zp, zq)
    near_y = (chip ^ 2, core, zp, zq)
    greet([partner, side, cross] + ([near_x, near_y] if with_mix else []), keep, moves)

    def quarter(ref, index):
        return ref.at[rows_at(index * part, part)]

    own_row = remote(tokens_ref.at[zq], quarter(row_ref, z), sems, 0, keep)
    own_shared = remote(tokens_ref.at[2], quarter(shared_ref, z), sems, 2, keep)
    stay_row = pltpu.make_async_copy(tokens_ref.at[zq], quarter(row_ref, z), local_sem.at[0])
    stay_shared = pltpu.make_async_copy(tokens_ref.at[2], quarter(shared_ref, z), local_sem.at[1])

    @pl.when(moves)
    def _():
        own_row.start()

    @pl.when(jnp.logical_not(moves))
    def _():
        stay_row.start()

    cross_row = remote(tokens_ref.at[1 - zq], quarter(row_ref, z), sems, 1, cross)
    cross_row.start()

    @pl.when(moves)
    def _():
        own_shared.start()

    @pl.when(jnp.logical_not(moves))
    def _():
        stay_shared.start()

    lens_copy = remote(lens_ref, lens_out.at[core], sems, 8, partner)
    lens_copy.start()
    lens_stay = pltpu.make_async_copy(lens_ref, lens_out.at[core], local_sem.at[2])
    lens_stay.start()
    if with_mix:
        shard = mix_ref.shape[1]

        def piece(index):
            return mix_out.at[rows_at(index * shard, shard)]

        mine, theirs = 2 * chip + core, 2 * chip + 1 - core
        x_mine, y_other = 2 * (chip ^ 1) + core, 2 * (chip ^ 2) + 1 - core

        def move(source, gain_source, index, at, device):
            copies = (
                remote(source, piece(index), sems, 9 + 2 * at, device),
                remote(gain_source, gains_out.at[index], sems, 10 + 2 * at, device),
            )
            for copy in copies:
                copy.start()
            return copies

        def arrived(copies):
            for copy in copies:
                copy.wait_recv()

        to_core = move(mix_ref.at[1 - core], gains_ref, mine, 0, partner)
        a_x = move(mix_ref.at[core], gains_ref, mine, 1, near_x)
        a_y = move(mix_ref.at[core], gains_ref, mine, 2, near_y)
        mix_stay = pltpu.make_async_copy(mix_ref.at[core], piece(mine), local_sem.at[3])
        mix_stay.start()
        gain_stay = pltpu.make_async_copy(gains_ref, gains_out.at[mine], local_sem.at[4])
        gain_stay.start()
        arrived(to_core)
        b_x = move(piece(theirs), gains_out.at[theirs], theirs, 3, near_x)
        b_y = move(piece(theirs), gains_out.at[theirs], theirs, 4, near_y)
        arrived(a_x)
        a_far = move(piece(x_mine), gains_out.at[x_mine], x_mine, 5, near_y)
        arrived(b_y)
        b_far = move(piece(y_other), gains_out.at[y_other], y_other, 6, near_x)

    @pl.when(moves)
    def _():
        own_row.wait_recv()

    @pl.when(jnp.logical_not(moves))
    def _():
        stay_row.wait()

    first, second = 2 * core + zq, 2 * core + 1 - zq
    row_one = remote(quarter(row_ref, first), quarter(row_ref, first), sems, 3, partner)
    row_one.start()
    cross_row.wait_recv()
    row_two = remote(quarter(row_ref, second), quarter(row_ref, second), sems, 4, partner)
    row_two.start()

    @pl.when(moves)
    def _():
        own_shared.wait_recv()

    @pl.when(jnp.logical_not(moves))
    def _():
        stay_shared.wait()

    to_side = remote(quarter(shared_ref, first), quarter(shared_ref, first), sems, 5, side)
    to_side.start()
    shared_one = remote(quarter(shared_ref, first), quarter(shared_ref, first), sems, 6, partner)
    shared_one.start()
    to_side.wait_recv()
    shared_two = remote(quarter(shared_ref, second), quarter(shared_ref, second), sems, 7, partner)
    shared_two.start()

    lens_copy.wait()
    lens_stay.wait()
    if with_mix:
        mix_stay.wait()
        gain_stay.wait()
        for copies in (a_y, b_x, a_far, b_far):
            arrived(copies)
        for copies in (to_core, a_x, a_y, b_x, b_y, a_far, b_far):
            for copy in copies:
                copy.wait_send()
    for copy in (row_one, row_two, shared_one, shared_two):
        copy.wait()
    to_side.wait_send()
    cross_row.wait_send()

    @pl.when(moves)
    def _():
        own_row.wait_send()
        own_shared.wait_send()


def gather_rows(tokens, lens, mix, gains, with_mix):
    _, part, model = tokens.shape
    pieces = mix.shape[1] * 8
    anywhere = pl.BlockSpec(memory_space=pl.ANY)
    return pl.pallas_call(
        functools.partial(gather_kernel, with_mix),
        in_specs=[anywhere] * 4,
        out_specs=[anywhere] * 5,
        out_shape=[
            jax.ShapeDtypeStruct((4 * part, model), BF16),
            jax.ShapeDtypeStruct((4 * part, model), BF16),
            jax.ShapeDtypeStruct((2,) + lens.shape, jnp.int32),
            jax.ShapeDtypeStruct((pieces, mix.shape[2]), BF16),
            jax.ShapeDtypeStruct((8,) + gains.shape, BF16),
        ],
        scratch_shapes=[
            pltpu.SemaphoreType.DMA((23,)),
            pltpu.SemaphoreType.DMA((23,)),
            pltpu.SemaphoreType.DMA((5,)),
        ],
        compiler_params=pltpu.CompilerParams(collective_id=0, has_side_effects=True),
        name="gather_rows",
    )(tokens, lens, mix, gains)


def to_tokens_kernel(row_ref, shared_ref, out_ref, sent, got, local_sem):
    chip, core, zp, zq = here()
    partner = (chip, 1 - core, zp, zq)
    half, width = row_ref.shape[0] // 2, row_ref.shape[1]
    part = half // 2
    greet([partner])
    lanes = pl.ds(pl.multiple_of(core * width, 128), width)
    top, bottom = out_ref.at[pl.ds(0, half), lanes], out_ref.at[pl.ds(half, part), lanes]
    copies = [
        remote(row_ref.at[rows_at((1 - core) * half, half)], top, (sent, got), 0, partner),
        remote(shared_ref.at[rows_at((1 - core) * part, part)], bottom, (sent, got), 1, partner),
        pltpu.make_async_copy(row_ref.at[rows_at(core * half, half)], top, local_sem.at[0]),
        pltpu.make_async_copy(shared_ref.at[rows_at(core * part, part)], bottom, local_sem.at[1]),
    ]
    for copy in copies:
        copy.start()
    for copy in copies:
        copy.wait()


def to_heads_kernel(grad_ref, row_ref, shared_ref, sent, got, local_sem):
    chip, core, zp, zq = here()
    partner = (chip, 1 - core, zp, zq)
    half, width = row_ref.shape[0] // 2, row_ref.shape[1]
    part = half // 2
    greet([partner])

    def source(first, count, side):
        return grad_ref.at[pl.ds(first, count), pl.ds(pl.multiple_of(side * width, 128), width)]

    top, bottom = row_ref.at[rows_at(core * half, half)], shared_ref.at[rows_at(core * part, part)]
    copies = [
        remote(source(0, half, 1 - core), top, (sent, got), 0, partner),
        remote(source(half, part, 1 - core), bottom, (sent, got), 1, partner),
        pltpu.make_async_copy(source(0, half, core), top, local_sem.at[0]),
        pltpu.make_async_copy(source(half, part, core), bottom, local_sem.at[1]),
    ]
    for copy in copies:
        copy.start()
    for copy in copies:
        copy.wait()


def core_exchange(kernel, ident, outs, *arrays):
    anywhere = pl.BlockSpec(memory_space=pl.ANY)
    return pl.pallas_call(
        kernel,
        in_specs=[anywhere] * len(arrays),
        out_specs=[anywhere] * len(outs),
        out_shape=[jax.ShapeDtypeStruct(shape, BF16) for shape in outs],
        scratch_shapes=[
            pltpu.SemaphoreType.DMA((2,)),
            pltpu.SemaphoreType.DMA((2,)),
            pltpu.SemaphoreType.DMA((2,)),
        ],
        compiler_params=pltpu.CompilerParams(collective_id=ident, has_side_effects=True),
        name="core_exchange",
    )(*arrays)


def finish_kernel(
    grad_ref, mix_ref, out_ref, total_ref, gains_ref,
    relay, final, core_got, chunks, gain_parts, chunk_got, gain_got, sent, got, local_sem,
):
    chip, core, zp, zq = here()
    z = 2 * zp + zq
    sems = (sent, got)
    part = out_ref.shape[1]
    shard = mix_ref.shape[1] - 16
    quarter = shard // 2
    columns = mix_ref.shape[2]
    partner = (chip, 1 - core, zp, zq)
    keep = (chip, zp, core, zq)
    cross = (chip, zp, core, 1 - zq)
    moves = core != zp
    near_x = (chip ^ 1, core, zp, zq)
    near_y = (chip ^ 2, core, zp, zq)
    along = [(chip, core, zp, 1 - zq), (chip, core, 1 - zp, zq), (chip, core, 1 - zp, 1 - zq)]
    greet([partner, cross, near_x, near_y] + along, keep, moves)

    mine, theirs = 2 * chip + core, 2 * chip + 1 - core
    x_mine, x_other = 2 * (chip ^ 1) + core, 2 * (chip ^ 1) + 1 - core
    y_mine, y_other = 2 * (chip ^ 2) + core, 2 * (chip ^ 2) + 1 - core
    far_mine, far_other = 2 * (chip ^ 3) + core, 2 * (chip ^ 3) + 1 - core
    first = remote(mix_ref.at[far_mine], relay.at[0], sems, 0, near_y)
    second = remote(mix_ref.at[far_other], relay.at[1], sems, 1, near_x)
    first.start()
    second.start()
    direct_x = remote(mix_ref.at[x_other], final.at[0], sems, 2, near_x)
    direct_y = remote(mix_ref.at[y_mine], final.at[1], sems, 3, near_y)
    direct_x.start()
    direct_y.start()

    own = pl.ds(pl.multiple_of(zq * part, 16), part)
    own_row = remote(grad_ref.at[own], out_ref.at[zq], sems, 4, keep)
    own_shared = remote(grad_ref.at[pl.ds(2 * part, part)], out_ref.at[2], sems, 5, keep)
    stay_row = pltpu.make_async_copy(grad_ref.at[own], out_ref.at[zq], local_sem.at[0])
    stay_shared = pltpu.make_async_copy(grad_ref.at[pl.ds(2 * part, part)], out_ref.at[2], local_sem.at[1])

    @pl.when(moves)
    def _():
        own_row.start()
        own_shared.start()

    @pl.when(jnp.logical_not(moves))
    def _():
        stay_row.start()
        stay_shared.start()

    cross_row = remote(grad_ref.at[rows_at((1 - zq) * part, part)], out_ref.at[zq], sems, 6, cross)
    cross_row.start()

    def add(*terms):
        total = terms[0].astype(F32)
        for term in terms[1:]:
            total = total + term.astype(F32)
        return total

    first.wait_recv()
    relay[2] = add(relay[0], mix_ref[x_mine]).astype(BF16)
    onward_x = remote(relay.at[2], final.at[2], sems, 7, near_x)
    onward_x.start()
    second.wait_recv()
    relay[3] = add(relay[1], mix_ref[y_other]).astype(BF16)
    onward_y = remote(relay.at[3], final.at[3], sems, 8, near_y)
    onward_y.start()
    direct_x.wait_recv()
    onward_y.wait_recv()
    relay[4] = add(mix_ref[theirs], final[0], final[3]).astype(BF16)
    to_core = remote(relay.at[4], core_got, sems, 9, partner)
    to_core.start()
    direct_y.wait_recv()
    onward_x.wait_recv()
    kept = add(mix_ref[mine], final[1], final[2])
    for i in range(2):
        chunks[2 * core + i] = kept[i * quarter : (i + 1) * quarter].astype(BF16)
    to_core.wait_recv()
    for i in range(2):
        chunks[2 * (1 - core) + i] = core_got[i * quarter : (i + 1) * quarter]
    gain_parts[0] = (kept[shard:] + core_got[shard:].astype(F32)).astype(BF16)
    hops = [z ^ 1, z ^ 2, z ^ 3]
    copies = []
    for i in range(3):
        copies.append(remote(chunks.at[hops[i]], chunk_got.at[i], sems, 10 + i, along[i]))
        copies.append(remote(gain_parts.at[0], gain_got.at[i], sems, 13 + i, along[i]))
    for copy in copies:
        copy.start()
    for copy in copies:
        copy.wait_recv()
    gains_ref[...] = add(gain_parts[0], gain_got[0], gain_got[1], gain_got[2])
    chunk_got[3] = add(chunks[z], chunk_got[0], chunk_got[1], chunk_got[2]).astype(BF16)
    spread = [remote(chunk_got.at[3], chunk_got.at[4 + i], sems, 16 + i, along[i]) for i in range(3)]
    for copy in spread:
        copy.start()

    def place(index, values):
        half, up = index // 2, index % 2
        third = columns // 3
        values = values.astype(F32)
        for h in range(2):
            for u in range(2):

                @pl.when((half == h) & (up == u))
                def _():
                    for p in range(3):
                        total_ref[u * quarter : (u + 1) * quarter, (2 * p + h) * third : (2 * p + h + 1) * third] = (
                            values[:, p * third : (p + 1) * third]
                        )

    place(z, chunk_got[3])
    for i in range(3):
        spread[i].wait_recv()
        place(hops[i], chunk_got[4 + i])
    for copy in copies + spread + [first, second, direct_x, direct_y, onward_x, onward_y, to_core]:
        copy.wait_send()
    cross_row.wait()

    @pl.when(moves)
    def _():
        own_row.wait()
        own_shared.wait()

    @pl.when(jnp.logical_not(moves))
    def _():
        stay_row.wait()
        stay_shared.wait()


def finish(grad, mix):
    tokens, model = grad.shape
    _, rows, columns = mix.shape
    shard = rows - 16
    anywhere = pl.BlockSpec(memory_space=pl.ANY)
    local_space = pl.BlockSpec(memory_space=pltpu.VMEM)
    buffers = lambda count, size: pltpu.VMEM((count, size, columns), BF16)
    return pl.pallas_call(
        finish_kernel,
        in_specs=[anywhere, local_space],
        out_specs=[anywhere, local_space, local_space],
        out_shape=[
            jax.ShapeDtypeStruct((3, tokens // 3, model), BF16),
            jax.ShapeDtypeStruct((shard, 2 * columns), F32),
            jax.ShapeDtypeStruct((16, columns), F32),
        ],
        scratch_shapes=[
            buffers(5, rows),
            buffers(4, rows),
            pltpu.VMEM((rows, columns), BF16),
            buffers(4, shard // 2),
            buffers(1, 16),
            buffers(7, shard // 2),
            buffers(3, 16),
            pltpu.SemaphoreType.DMA((19,)),
            pltpu.SemaphoreType.DMA((19,)),
            pltpu.SemaphoreType.DMA((2,)),
        ],
        compiler_params=pltpu.CompilerParams(
            collective_id=3, has_side_effects=True, vmem_limit_bytes=VMEM_LIMIT
        ),
        name="finish",
    )(grad, mix)


def row_bounds(lengths_row, length):
    pics = lengths_row.shape[0]
    ends = jnp.cumsum(lengths_row)
    starts = ends - lengths_row
    last = jnp.arange(pics) == jnp.sum(lengths_row > 0) - 1
    table = jnp.stack([starts, ends, jnp.where(last, length, ends)]).astype(jnp.int32)
    table = jnp.pad(table, ((0, 5), (0, HEAD - pics)), constant_values=2 * length)
    return jnp.tile(table, (1, 2)), ends[-1]


def local(
    tokens, lengths, pictures, first_gain, mix_weight, query_gain, key_gain, out_weight,
    second_gain, up_weight, down_weight, cotangent,
):
    chip, core, zp, zq = here()
    chips = lax.axis_size("chip")
    square = chips == 4
    rows = ("chip", "core")
    _, part, model = tokens.shape
    length = 4 * part
    half = 2 * part
    width = HEADS // 2 * HEAD
    pics = lengths.shape[1]
    shard = mix_weight.shape[0]

    gains = jnp.stack([first_gain, query_gain, key_gain, second_gain])
    gains = jnp.pad(gains, ((0, 12), (0, 128 - shard)))
    mix_split = mix_weight.reshape(shard, 3, 2, width).transpose(2, 0, 1, 3).reshape(2, shard, 3 * width)
    lens = jnp.pad(lengths, ((0, 5), (0, 128 - pics)))
    row_tokens, shared_tokens, lens, mix_half, gain_parts = gather_rows(tokens, lens, mix_split, gains, square)
    if not square:
        whole = lax.all_gather(mix_weight, rows, axis=0, tiled=True)
        mix_half = pick(whole.reshape(model, 3, 2, width), core, 2).reshape(model, 3 * width)
        gain_parts = lax.all_gather(gains, rows, axis=0, tiled=False)
    out_matrix = lax.all_gather(out_weight, rows, axis=0, tiled=True)
    up_matrix = lax.all_gather(up_weight, rows, axis=0, tiled=True)
    down_matrix = lax.all_gather(down_weight, rows, axis=0, tiled=True)
    gains = gain_parts[:, :4, :shard].transpose(1, 0, 2).reshape(4, 1, model).astype(F32)
    gain_first, gain_second = gains[0], gains[3]
    gain_query = pick(gains[1].reshape(2, 1, width), core)
    gain_key = pick(gains[2].reshape(2, 1, width), core)
    owner_lengths = pick(lens, zp)[:3, :pics]
    bounds, filled = row_bounds(pick(owner_lengths, zq), length)
    shared_bounds, shared_filled = row_bounds(owner_lengths[2], length)

    def spread(array):
        mine = lax.ppermute(pick(array, zq), COLUMN, KEEP)
        cross = lax.ppermute(pick(array, 1 - zq), COLUMN, CROSS)
        shared = lax.ppermute(array[2], COLUMN, KEEP)
        return jnp.concatenate([jnp.where(zq == 0, mine, cross), jnp.where(zq == 0, cross, mine), shared])

    def collect(array):
        first, second, shared = array[:part], array[part:half], array[half:]
        mine = lax.ppermute(jnp.where(zq == 0, first, second), COLUMN, KEEP)
        cross = lax.ppermute(jnp.where(zq == 0, second, first), COLUMN, CROSS)
        shared = lax.ppermute(shared, COLUMN, KEEP)
        return jnp.stack([jnp.where(zq == 0, mine, cross), jnp.where(zq == 0, cross, mine), shared])

    grad_tokens = spread(cotangent)

    normed, q, k, v, raw = project(row_tokens, gain_first, mix_half, gain_query, gain_key)
    out, aug = attend(q, k, v, bounds, pics, length)
    shared_normed, shared_q, shared_k, shared_v, shared_raw = project(
        shared_tokens, gain_first, mix_half, gain_query, gain_key
    )
    shared_out, shared_aug = attend(shared_q, shared_k, shared_v, shared_bounds, pics, half)
    (attended,) = core_exchange(to_tokens_kernel, 1, [(3 * part, model)], out, shared_out)

    own_tokens = jnp.concatenate(
        [
            lax.dynamic_slice_in_dim(row_tokens, core * half, half),
            lax.dynamic_slice_in_dim(shared_tokens, (2 * core + zq) * part, part),
        ]
    )
    place = core * half + jnp.arange(half)
    shared_place = (2 * core + zq) * part + jnp.arange(part)
    valid = jnp.concatenate([place < filled, shared_place < shared_filled])
    grad_low = jnp.where(valid[:, None], grad_tokens, 0)
    output, middle_grad, attended_grad, out_grad, up_grad, down_grad, second_gain_grad = dense(
        attended, own_tokens, out_matrix, gain_second, grad_low, up_matrix, down_matrix
    )
    output = collect(output)

    def reduce(grad):
        return lax.psum(lax.psum_scatter(grad, rows, scatter_dimension=0, tiled=True), SEQ).astype(F32)

    up_out = reduce(up_grad)
    down_out = reduce(down_grad)
    outw_out = reduce(out_grad)

    grad, shared_grad = core_exchange(to_heads_kernel, 2, [(length, width), (half, width)], attended_grad)
    shared_dq, part_k, part_v, shared_qgg, _ = attend_back(
        shared_aug, shared_k, shared_v, shared_out, shared_grad, shared_raw, gain_query, gain_key,
        shared_bounds, pics,
    )

    def to_side(array):
        return swap(pick(array.reshape(2, 2, part, width), 1 - zq, 1), "zq").reshape(half, width)

    got_k, got_v = to_side(part_k), to_side(part_v)
    dq, dk, dv, qgg, kgg = attend_back(
        aug, k, v, out, grad, raw, gain_query, gain_key, bounds, pics
    )
    shared_dk, shared_dv, shared_kgg = shared_keys(part_k, part_v, got_k, got_v, shared_raw, gain_key)
    mixed = jnp.concatenate(
        [jnp.concatenate([dq, shared_dq]), jnp.concatenate([dk, shared_dk]), jnp.concatenate([dv, shared_dv])],
        axis=1,
    )
    own_shared = pick(shared_normed.reshape(2, 2, part, model), zq, 1).reshape(half, model)
    mix_grad = tn(jnp.concatenate([normed, own_shared]), mixed).astype(BF16)
    partial = nt(mixed, mix_half)
    row_partial = partial[:length].reshape(2, half, model)
    shared_partial = partial[length:].reshape(2, part, model)
    mine = jnp.concatenate([pick(row_partial, core), pick(shared_partial, core)])
    sent = jnp.concatenate([pick(row_partial, 1 - core), pick(shared_partial, 1 - core)])
    normed_grad = mine + swap(sent.astype(BF16), "core").astype(F32)
    n_first, r_first = norm_parts(own_tokens.astype(F32))
    input_part, first_gain_grad = norm_back(normed_grad, n_first, r_first, gain_first)
    input_grad = (middle_grad + input_part).astype(BF16)

    def place_heads(values):
        return jnp.where(jnp.arange(2)[:, None] == core, values, 0.0).reshape(1, model)

    gain_grads = jnp.concatenate(
        [first_gain_grad, place_heads(qgg + shared_qgg), place_heads(kgg + shared_kgg), second_gain_grad]
    )
    gain_grads = gain_grads.reshape(4, 2 * chips, shard).transpose(1, 0, 2).astype(BF16)
    if square:
        gain_rows = jnp.pad(gain_grads, ((0, 0), (0, 12), (0, 3 * width - shard)))
        payload = jnp.concatenate([mix_grad.reshape(2 * chips, shard, 3 * width), gain_rows], axis=1)
        input_out, mix_out, gains_out = finish(input_grad, payload)
        gains_out = gains_out[:4, :shard]
    else:
        input_out = collect(input_grad)
        spread_mix = jnp.where(
            jnp.arange(2)[None, None, :, None] == core, mix_grad.reshape(model, 3, 1, width), 0
        ).reshape(model, 6 * width)
        mix_out = reduce(spread_mix)
        gains_out = reduce(gain_grads).reshape(4, shard)
    return (
        output, input_out, gains_out[0], mix_out, gains_out[1], gains_out[2], outw_out, gains_out[3],
        up_out, down_out,
    )


def solution(mesh):
    fsdp = mesh.shape["fsdp"]
    split = Mesh(mesh.devices.reshape(fsdp // 2, 2, 2, 2), ("chip", "core", "zp", "zq"))
    rows = ("chip", "core")
    return jax.shard_map(
        local,
        mesh=split,
        in_specs=(
            P(rows, SEQ, None),
            P(rows, None),
            P(rows, SEQ),
            P(rows),
            P(rows, None),
            P(rows),
            P(rows),
            P(rows, None),
            P(rows),
            P(rows, None),
            P(rows, None),
            P(rows, SEQ, None),
        ),
        out_specs=(
            P(rows, SEQ, None),
            P(rows, SEQ, None),
            P(rows),
            P(rows, None),
            P(rows),
            P(rows),
            P(rows, None),
            P(rows),
            P(rows, None),
            P(rows, None),
        ),
        check_vma=False,
    )
```

time: 690 us -> 469 us (0.68)
  starting transfers between devices: 171 us -> 21.6 us
  Pallas kernels: 215 us -> 306 us
  local copies, waits for them, and re-layouts: 91 us -> 31.1 us
  other arithmetic: 89.4 us -> 30.2 us
  waiting for transfers between devices: 93.1 us -> 36.6 us
  between operations: 4.58 us -> 16.5 us
    ppermute x74 -> x3, starting transfers between devices: 153 us -> 3.36 us  [swap(): return lax.ppermute(array, name, [(i, i ^ bit) for i in range(count)])]
    pallas_call x5 -> x10, Pallas kernels: 198 us -> 289 us  [the longest x1 92.9 us: finish(): pl.pallas_call(finish_kernel, in_specs=[anywhere, local_space], out_specs...]
    ppermute x74 -> x3, waiting for transfers between devices: 86 us -> 0.01 us  [swap(): return lax.ppermute(array, name, [(i, i ^ bit) for i in range(count)])]
    reduce_scatter x0 -> x3, waiting for transfers between devices: none -> 33.7 us  [reduce(): lax.psum_scatter(grad, rows, scatter_dimension=0, tiled=True)]
    reshape x14 -> x4, local copies, waits for them, and re-layouts: 17.7 us -> 1.47 us  [the longest x3 1.47 us: local(): mix_weight.reshape(shard, 3, 2, width).transpose(2, 0, 1, 3)]
    concatenate x30 -> x3, other arithmetic: 19.6 us -> 4.06 us  [the longest x1 2.96 us: local(): jnp.concatenate([mix_grad.reshape(2 * chips, shard, 3 * width), gain_rows...]
    convert_element_type x32 -> x6, other arithmetic: 23.6 us -> 9.09 us  [the longest x3 4.97 us: reduce(): lax.psum(lax.psum_scatter(grad, rows, scatter_dimension=0, tiled=True), SEQ)]
    squeeze x32 -> x9, local copies, waits for them, and re-layouts: 19 us -> 7.57 us  [pick(): return lax.dynamic_index_in_dim(array, index, axis, keepdims=False)]
  transfers between devices with their start and end apart: 86 -> 16, of which waited for: 22 -> 1; matrix products, arithmetic and copies ran while one was open for 25% -> 15% of each run, Pallas kernels for 27% -> 58%
where the time goes in v2:
time: 469 us; the launch traced here: 461 us
  Pallas kernels  306 us (65%)
  waiting for transfers between devices  36.6 us (8%)
  local copies, waits for them, and re-layouts  31.1 us (7%)
  other arithmetic  30.2 us (6%)
  starting transfers between devices  21.6 us (5%)
  matrix products  18.1 us (4%)
  between operations  16.5 us (4%)
    pallas_call x1, Pallas kernels, finish(): pl.pallas_call(finish_kernel, in_specs=[anywhere, local_space], out_specs...  92.9 us
    pallas_call x1, Pallas kernels, gather_rows(): pl.pallas_call(functools.partial(gather_kernel, with_mix), in_specs=[anyw...  53 us
    pallas_call x2, Pallas kernels, attend_back(): pl.pallas_call(functools.partial(attend_back_kernel, pics), grid=(pairs,)...  41.1 us
    pallas_call x2, Pallas kernels, core_exchange(): pl.pallas_call(kernel, in_specs=[anywhere] * len(arrays), out_specs=[anyw...  39.5 us
    pallas_call x1, Pallas kernels, dense(): pl.pallas_call(dense_kernel, grid=(hidden // tile,), in_specs=[whole, who...  39.2 us
    reduce_scatter x3, waiting for transfers between devices, reduce(): lax.psum_scatter(grad, rows, scatter_dimension=0, tiled=True)  33.7 us
    pallas_call x2, Pallas kernels, attend(): pl.pallas_call(functools.partial(attend_kernel, pics), grid=(pairs,), in_...  18.1 us
    pallas_call x2, Pallas kernels, project(): pl.pallas_call(project_kernel, grid=(tokens // BLOCK,), in_specs=[rows(mo...  17.5 us
  transfers between devices with their start and end apart: 16, of which 1 were waited for; matrix products, arithmetic and copies ran while one was open for 15% of the time, Pallas kernels for 58%

profile of v2, /device:TPU:0, one launch (start us, length us, event | category | flops | bytes accessed | tf_op | source)
XLA Modules:
  0.0 460.5 jit_solution(18247935222617722985)
XLA Ops:
  13.4 4.5 collective-permute-start.2
  17.9 3.0 collective-permute-start.1
  23.6 53.0 %gather_rows.1 = (bf16[1024,768]{1,0:T(8,128)(2,1)}, bf16[1024,768]{1,0:T(8,128)(2,1)}, s32[2,8,128]{2,1,0:T(8,128)}, bf16[768,1152]{1,0:T(8,128)(2,1)}, bf16[8,16,128]{2,1,0:T(8,128)(2,1)}) custom-call(bf16[3,256,768]{2,1,0:T(8,128)(2,1)} %tokens_ref.1, s32[8,128]{1,0:T(8,128)} %pad.19.lens_ref, bf16[2,96,1152]{2,1,0:T(8,128)(2,1)} %reshape.266.mix_ref, ...), custom_call_target="tpu_custom_call" | custom-call | tf_op jit(solution)/shard_map/gather_rows/pallas_call | solution.py:656
  85.8 8.8 %project.2 = (bf16[1024,768]{1,0:T(8,128)(2,1)}, bf16[1024,384]{1,0:T(8,128)(2,1)}, bf16[1024,384]{1,0:T(8,128)(2,1)}, bf16[1024,384]{1,0:T(8,128)(2,1)}, f32[1024,768]{1,0:T(8,128)}) custom-call(bf16[1024,768]{1,0:T(8,128)(2,1)} %get-tuple-element.53.x_ref, f32[1,768]{1,0:T(1,128)} %squeeze.73.gain_ref, bf16[768,1152]{1,0:T(8,128)(2,1)} %get-tuple-element.55.weight_ref, ...), custom_call_target="tpu_custom_call" | custom-call | flops 1811939328 | bytes 9437184 | tf_op jit(solution)/shard_map/project/pallas_call | solution.py:78
  94.5 8.7 %project.3 = (bf16[1024,768]{1,0:T(8,128)(2,1)}, bf16[1024,384]{1,0:T(8,128)(2,1)}, bf16[1024,384]{1,0:T(8,128)(2,1)}, bf16[1024,384]{1,0:T(8,128)(2,1)}, f32[1024,768]{1,0:T(8,128)}) custom-call(bf16[1024,768]{1,0:T(8,128)(2,1)} %get-tuple-element.61.x_ref, f32[1,768]{1,0:T(1,128)} %squeeze.73.gain_ref, bf16[768,1152]{1,0:T(8,128)(2,1)} %get-tuple-element.55.weight_ref, ...), custom_call_target="tpu_custom_call" | custom-call | flops 1811939328 | bytes 9437184 | tf_op jit(solution)/shard_map/project/pallas_call | solution.py:78
  103.3 7.0 %attend.3 = (bf16[512,384]{1,0:T(8,128)(2,1)}, bf16[6,512,128]{2,1,0:T(8,128)(2,1)}) custom-call(bf16[1024,384]{1,0:T(8,128)(2,1)} %get-tuple-element.62.q_ref, bf16[1024,384]{1,0:T(8,128)(2,1)} %get-tuple-element.63.k_ref, bf16[1024,384]{1,0:T(8,128)(2,1)} %get-tuple-element.64.v_ref, s32[8,128]{1,0:T(8,128)} %tile.21.bounds_ref), custom_call_target="tpu_custom_call" | custom-call | flops 3221225472 | bytes 4718592 | tf_op jit(solution)/shard_map/attend/pallas_call | solution.py:188
  110.3 11.1 %attend.2 = (bf16[1024,384]{1,0:T(8,128)(2,1)}, bf16[6,1024,128]{2,1,0:T(8,128)(2,1)}) custom-call(bf16[1024,384]{1,0:T(8,128)(2,1)} %get-tuple-element.56.q_ref, bf16[1024,384]{1,0:T(8,128)(2,1)} %get-tuple-element.57.k_ref, bf16[1024,384]{1,0:T(8,128)(2,1)} %get-tuple-element.58.v_ref, s32[8,128]{1,0:T(8,128)} %tile.9.bounds_ref), custom_call_target="tpu_custom_call" | custom-call | flops 6442450944 | bytes 4718592 | tf_op jit(solution)/shard_map/attend/pallas_call | solution.py:188
  121.4 19.2 %core_exchange.2.attended_ref = bf16[768,768]{1,0:T(8,128)(2,1)} custom-call(bf16[1024,384]{1,0:T(8,128)(2,1)} %get-tuple-element.60.row_ref.out_ref, bf16[512,384]{1,0:T(8,128)(2,1)} %get-tuple-element.65.shared_ref.out_ref), custom_call_target="tpu_custom_call" | custom-call | tf_op jit(solution)/shard_map/core_exchange/pallas_call | solution.py:722
  144.2 2.3 maximum_select_fusion.grad_ref
  146.5 39.2 %dense.1 = (bf16[768,768]{1,0:T(8,128)(2,1)}, f32[768,768]{1,0:T(8,128)}, bf16[768,768]{1,0:T(8,128)(2,1)}, bf16[768,768]{1,0:T(8,128)(2,1)}, bf16[768,3072]{1,0...) custom-call(bf16[768,768]{1,0:T(8,128)(2,1)} %core_exchange.2.attended_ref, ...), custom_call_target="tpu_custom_call" | custom-call | flops 28991029248 | bytes 18874368 | tf_op jit(solution)/shard_map/dense/pallas_call | solution.py:453
  192.0 4.5 collective-permute-start.3
  197.2 3.6 collective-permute-start.4
  200.8 20.3 %core_exchange.3 = (bf16[1024,384]{1,0:T(8,128)(2,1)}, bf16[512,384]{1,0:T(8,128)(2,1)}) custom-call(bf16[768,768]{1,0:T(8,128)(2,1)} %get-tuple-element.69.grad_ref), custom_call_target="tpu_custom_call" | custom-call | tf_op jit(solution)/shard_map/core_exchange/pallas_call | solution.py:722
  221.1 13.7 %attend_back.3 = (bf16[512,384]{1,0:T(8,128)(2,1)}, bf16[1024,384]{1,0:T(8,128)(2,1)}, bf16[1024,384]{1,0:T(8,128)(2,1)}, f32[1,384]{1,0:T(1,128)}, f32[1,384]{1,0:T(1,128)}) custom-call(bf16[6,512,128]{2,1,0:T(8,128)(2,1)} %get-tuple-element.73.aug_ref, bf16[1024,384]{1,0:T(8,128)(2,1)} %get-tuple-element.63.k_ref, ...), custom_call_target="tpu_custom_call" | custom-call | flops 8053063680 | bytes 7864320 | tf_op jit(solution)/shard_map/attend_back/pallas_call | solution.py:299
  235.9 3.2 collective-permute-start.6
  240.3 27.4 %attend_back.2 = (bf16[1024,384]{1,0:T(8,128)(2,1)}, bf16[1024,384]{1,0:T(8,128)(2,1)}, bf16[1024,384]{1,0:T(8,128)(2,1)}, f32[1,384]{1,0:T(1,128)}, f32[1,384]{1,0:T(1,128)}) custom-call(bf16[6,1024,128]{2,1,0:T(8,128)(2,1)} %get-tuple-element.68.aug_ref, bf16[1024,384]{1,0:T(8,128)(2,1)} %get-tuple-element.57.k_ref, ...), custom_call_target="tpu_custom_call" | custom-call | flops 16106127360 | bytes 7864320 | tf_op jit(solution)/shard_map/attend_back/pallas_call | solution.py:299
  270.6 5.1 %shared_keys.1 = (bf16[512,384]{1,0:T(8,128)(2,1)}, bf16[512,384]{1,0:T(8,128)(2,1)}, f32[1,384]{1,0:T(1,128)}) custom-call(bf16[1024,384]{1,0:T(8,128)(2,1)} %get-tuple-element.78.dk_ref, bf16[1024,384]{1,0:T(8,128)(2,1)} %get-tuple-element.79.dv_ref, bf16[512,384]{1,0:T(8,128)(2,1)} %bitcast.83, bf16[512,384]{1,0:T(8,128)(2,1)} %bitcast.84, ...), custom_call_target="tpu_custom_call" | custom-call | tf_op jit(solution)/shard_map/shared_keys/pallas_call | solution.py:358
  275.7 13.6 %fusion.39 = f32[1536,768]{1,0:T(8,128)S(1)} fusion(bf16[768,1152]{1,0:T(8,128)(2,1)S(1)} %copy-done.26, bf16[512,384]{1,0:T(8,128)(2,1)} %get-tuple-element.82, bf16[1024,384]{1,0:T(8,128)(2,1)S(1)} %copy-done.34, bf16[512,384]{1,0:T(8,128)(2,1)} %get-tuple-element.80, bf16[1024,384]{1,0:T(8,128)(2,1)S(1)} %copy-done.32, ...), kind=kOutput, calls=%fused_computation.107 | convolution fusion | flops 2739142656 | bytes 10027008 | tf_op jit(solution)/shard_map/dot_general | solution.py:105
  300.9 4.6 convolution_convert_fusion
  306.5 2.5 fusion.11
  309.1 33.7 %reduce-scatter.8.cloned.1.call-done = bf16[384,768]{1,0:T(8,128)(2,1)} async-done(((bf16[3072,768]{1,0:T(8,128)(2,1)}), bf16[384,768]{1,0:T(8,128)(2,1)}) %reduce-scatter.8.cloned.1.call-update) | async-done | bytes 589840 | tf_op jit(solution)/shard_map/reduce_scatter | solution.py:984
  346.6 3.0 fusion.16.mix_ref
  349.6 2.5 fusion.10.grad_ref
  352.1 92.9 %finish.1 = (bf16[3,256,768]{2,1,0:T(8,128)(2,1)}, f32[96,2304]{1,0:T(8,128)}, f32[16,1152]{1,0:T(8,128)}) custom-call(bf16[768,768]{1,0:T(8,128)(2,1)} %fusion.10.grad_ref, bf16[8,112,1152]{2,1,0:T(8,128)(2,1)} %fusion.16.mix_ref), custom_call_target="tpu_custom_call" | custom-call | tf_op jit(solution)/shard_map/finish/pallas_call | solution.py:872
  (188 shorter events, 56.7 us)
Async XLA Ops:
  7.2 13.8 %copy-start.17 = (s32[3,10]{1,0:T(4,128)S(1)}, s32[3,10]{1,0:T(4,128)}, u32[]{:S(2)}) copy-start(s32[3,10]{1,0:T(4,128)} %param.13) | copy-start | bytes 364
  7.2 14.3 %copy-start.11 = (bf16[96,2304]{1,0:T(8,128)(2,1)S(1)}, bf16[96,2304]{1,0:T(8,128)(2,1)}, u32[]{:S(2)}) copy-start(bf16[96,2304]{1,0:T(8,128)(2,1)} %param.15) | copy-start | bytes 1327108
  7.2 139.3 %all-gather.4.cloned.1.call-start = ((), (), s32[]{:S(2)}) async-start(), calls=%async_computation.3 | async-start | bytes 1327104 | tf_op jit(solution)/shard_map/all_gather | solution.py:934
  7.9 138.6 %all-gather.6.cloned.1.call-start = ((), (), s32[]{:S(2)}) async-start(), calls=%async_computation.4 | async-start | bytes 5308416 | tf_op jit(solution)/shard_map/all_gather | solution.py:935
  8.7 137.9 %all-gather.8.cloned.1.call-start = ((), (), s32[]{:S(2)}) async-start(), calls=%async_computation.5 | async-start | bytes 5308416 | tf_op jit(solution)/shard_map/all_gather | solution.py:936
  9.4 299.7 %reduce-scatter.4.cloned.1.call-start = ((), (), s32[]{:S(2)}) async-start(), calls=%async_computation.6 | async-start | bytes 1327104 | tf_op jit(solution)/shard_map/reduce_scatter | solution.py:984
  9.5 13.6 %copy-start.21 = (bf16[96]{0:T(256)(128)(2,1)S(1)}, bf16[96]{0:T(256)(128)(2,1)}, u32[]{:S(2)}) copy-start(bf16[96]{0:T(256)(128)(2,1)} %param.19) | copy-start | bytes 580
  9.5 13.5 %copy-start.22 = (bf16[96]{0:T(256)(128)(2,1)S(1)}, bf16[96]{0:T(256)(128)(2,1)}, u32[]{:S(2)}) copy-start(bf16[96]{0:T(256)(128)(2,1)} %param.17) | copy-start | bytes 580
  9.5 13.5 %copy-start.23 = (bf16[96]{0:T(256)(128)(2,1)S(1)}, bf16[96]{0:T(256)(128)(2,1)}, u32[]{:S(2)}) copy-start(bf16[96]{0:T(256)(128)(2,1)} %param.16) | copy-start | bytes 580
  9.5 13.5 %copy-start.24 = (bf16[96]{0:T(256)(128)(2,1)S(1)}, bf16[96]{0:T(256)(128)(2,1)}, u32[]{:S(2)}) copy-start(bf16[96]{0:T(256)(128)(2,1)} %param.14) | copy-start | bytes 580
  11.8 132.4 %collective-permute-start = (bf16[256,768]{1,0:T(8,128)(2,1)}, bf16[256,768]{1,0:T(8,128)(2,1)S(1)}, u32[]{:S(2)}, u32[]{:S(2)}) collective-permute-start(bf16[256,768]{1,0:T(8,128)(2,1)} %get-tuple-element.109), channel_id=1, source_target_pairs={{0,0},{1,1},{2,4},{3,5},{4,2},{5,3},{6,6},{7,7},{8,8},{9,9},{10,12... | collective-permute-start | bytes 1179656 | tf_op jit(solution)/shard_map/ppermute | solution.py:946
  13.4 130.8 %collective-permute-start.2 = (bf16[256,768]{1,0:T(8,128)(2,1)}, bf16[256,768]{1,0:T(8,128)(2,1)}, u32[]{:S(2)}, u32[]{:S(2)}) collective-permute-start(bf16[256,768]{1,0:T(8,128)(2,1)} %get-tuple-element.110), channel_id=1, source_target_pairs={{0,0},{1,1},{2,4},{3,5},{4,2},{5,3},{6,6},{7,7},{8,8},{9,9},{10,12... | collective-permute-start | bytes 1179656 | tf_op jit(solution)/shard_map/ppermute | solution.py:948
  17.9 126.3 %collective-permute-start.1 = (bf16[256,768]{1,0:T(8,128)(2,1)}, bf16[256,768]{1,0:T(8,128)(2,1)S(1)}, u32[]{:S(2)}, u32[]{:S(2)}) collective-permute-start(bf16[256,768]{1,0:T(8,128)(2,1)} %get-tuple-element.111), channel_id=1, source_target_pairs={{0,1},{1,0},{2,5},{3,4},{4,3},{5,2},{6,7},{7,6},{8,9},{9,8},{10,13... | collective-permute-start | bytes 1179656 | tf_op jit(solution)/shard_map/ppermute | solution.py:947
  121.4 21.6 %copy-start.14 = (bf16[1024,768]{1,0:T(8,128)(2,1)S(1)}, bf16[1024,768]{1,0:T(8,128)(2,1)}, u32[]{:S(2)}) copy-start(bf16[1024,768]{1,0:T(8,128)(2,1)} %get-tuple-element.53.x_ref) | copy-start | bytes 4718596
  185.8 123.3 %reduce-scatter.6.cloned.1.call-start = ((), (), s32[]{:S(2)}) async-start(), calls=%async_computation.7 | async-start | bytes 5308416 | tf_op jit(solution)/shard_map/reduce_scatter | solution.py:984
  186.4 156.4 %reduce-scatter.8.cloned.1.call-start = ((), (), s32[]{:S(2)}) async-start(), calls=%async_computation.8 | async-start | bytes 5308416 | tf_op jit(solution)/shard_map/reduce_scatter | solution.py:984
  187.0 259.4 %all-reduce.8.cloned.1.call-start = ((), (), s32[]{:S(2)}) async-start(), calls=%async_computation.9 | async-start | bytes 2654208 | tf_op jit(solution)/shard_map/psum | solution.py:984
  192.0 103.3 %collective-permute-start.3 = (bf16[256,768]{1,0:T(8,128)(2,1)}, bf16[256,768]{1,0:T(8,128)(2,1)}, u32[]{:S(2)}, u32[]{:S(2)}) collective-permute-start(bf16[256,768]{1,0:T(8,128)(2,1)} %get-tuple-element.106), channel_id=1, source_target_pairs={{0,0},{1,1},{2,4},{3,5},{4,2},{5,3},{6,6},{7,7},{8,8},{9,9},{10,12... | collective-permute-start | bytes 1179656 | tf_op jit(solution)/shard_map/ppermute | solution.py:953
  196.5 100.4 %collective-permute-start.5 = (bf16[256,768]{1,0:T(8,128)(2,1)S(1)}, bf16[256,768]{1,0:T(8,128)(2,1)S(1)}, u32[]{:S(2)}, u32[]{:S(2)}) collective-permute-start(bf16[256,768]{1,0:T(8,128)(2,1)S(1)} %get-tuple-element.107), channel_id=1, source_target_pairs={{0,0},{1,1},{2,4},{3,5},{4,2},{5,3},{6,6},{7,7},{8,8},{9,9},{10,12... | collective-permute-start | bytes 1179656 | tf_op jit(solution)/shard_map/ppermute | solution.py:955
  197.2 98.2 %collective-permute-start.4 = (bf16[256,768]{1,0:T(8,128)(2,1)}, bf16[256,768]{1,0:T(8,128)(2,1)}, u32[]{:S(2)}, u32[]{:S(2)}) collective-permute-start(bf16[256,768]{1,0:T(8,128)(2,1)} %get-tuple-element.108), channel_id=1, source_target_pairs={{0,1},{1,0},{2,5},{3,4},{4,3},{5,2},{6,7},{7,6},{8,9},{9,8},{10,13... | collective-permute-start | bytes 1179656 | tf_op jit(solution)/shard_map/ppermute | solution.py:954
  235.9 33.8 %collective-permute-start.6 = (bf16[2,256,384]{2,1,0:T(8,128)(2,1)S(1)}, bf16[2,256,384]{2,1,0:T(8,128)(2,1)S(1)}, u32[]{:S(2)}, u32[]{:S(2)}) collective-permute-start(bf16[2,256,384]{2,1,0:T(8,128)(2,1)S(1)} %dynamic-slice_bitcast_fusion.3), channel_id=1, source_target_pairs={{0,1},{1,0},{2,3},{3,2},{4,5},{5,4},{6,7},{7,6},{8,9},{9,8},{10,11... | collective-permute-start | bytes 1179656 | tf_op jit(solution)/shard_map/ppermute | solution.py:33
  240.2 29.5 %collective-permute-start.7 = (bf16[2,256,384]{2,1,0:T(8,128)(2,1)S(1)}, bf16[2,256,384]{2,1,0:T(8,128)(2,1)S(1)}, u32[]{:S(2)}, u32[]{:S(2)}) collective-permute-start(bf16[2,256,384]{2,1,0:T(8,128)(2,1)S(1)} %dynamic-slice_bitcast_fusion.2), channel_id=1, source_target_pairs={{0,1},{1,0},{2,3},{3,2},{4,5},{5,4},{6,7},{7,6},{8,9},{9,8},{10,11... | collective-permute-start | bytes 1179656 | tf_op jit(solution)/shard_map/ppermute | solution.py:33
  240.3 27.4 %copy-start.19 = (f32[1,384]{1,0:T(1,128)S(1)}, f32[1,384]{1,0:T(1,128)}, u32[]{:S(2)}) copy-start(f32[1,384]{1,0:T(1,128)} %get-tuple-element.86) | copy-start | bytes 4612
  295.2 10.3 %collective-permute-start.8 = (bf16[768,768]{1,0:T(8,128)(2,1)S(1)}, bf16[768,768]{1,0:T(8,128)(2,1)S(1)}, u32[]{:S(2)}, u32[]{:S(2)}) collective-permute-start(bf16[768,768]{1,0:T(8,128)(2,1)S(1)} %pad_maximum_fusion.2), channel_id=1, source_target_pairs={{0,4},{4,0},{1,5},{5,1},{2,6},{6,2},{3,7},{7,3},{8,12},{12,8},{9,1... | collective-permute-start | bytes 3538952 | tf_op jit(solution)/shard_map/ppermute | solution.py:33
  (30 other events, 102.2 us)
Sparse Core Ops, SparseCore 0:
  9.9 30.0 all-gather.3
  41.9 38.8 all-gather.5
  82.7 38.9 all-gather.7
  185.9 40.4 reduce-scatter.3
  230.0 53.8 reduce-scatter.5
  287.3 55.4 reduce-scatter.7
  345.5 88.0 all-reduce.7
